TPU v7x, 32 devices: a whole 2x2x4 slice. The times are simulated.
32 devices in a mesh: pipe: 4 (over y, x), ctx: 4 (over z), tp: 2 (over core).
Axes of the slice: x: 2, y: 2, z: 4, core: 2. Of those that a mesh axis runs over, the one named last changes fastest.
Arguments:
- q_self: bfloat16 [4, 1024, 4096], P('pipe', 'ctx', 'tp'), may hold values from -5 to 5
- kv_self: bfloat16 [4, 1024, 2, 512], P('pipe', 'ctx', None, 'tp'), may hold values from -5 to 5
- q_cross: bfloat16 [4, 1024, 4096], P('pipe', 'ctx', 'tp'), may hold values from -5 to 5
- kv_cross: bfloat16 [4, 2, 1024, 2, 512], P(None, None, ('pipe', 'ctx'), None, 'tp'), may hold values from -5 to 5
- sample_lengths: int32 [4, 8], P('pipe'), may hold values from 1 to 640, 1024 in all within a row
- sample_image: int32 [4, 8], P('pipe'), may hold values from 0 to 1
Outputs:
- self_out: bfloat16 [4, 1024, 4096], P('pipe', 'ctx', 'tp')
- cross_out: bfloat16 [4, 1024, 4096], P('pipe', 'ctx', 'tp')
Inputs may be any that keep to these rules, and one draw needn't show every extreme that they name: `sample_lengths`: each micro-batch's lengths sum to 1024; the longest sample of each micro-batch has exactly 640 positions.
All inputs are finite; a program needn't handle non-finite values.
Results may differ from a plain program's by a relative error of at most 0.0047.
Values may be sent and summed in bfloat16 or wider, within the bound.
No kernel may reach another device: no remote copies, remote signals or barrier semaphores. Data moves between devices by JAX's collectives and lax.ppermute only.
A program may use at most 128 MiB of HBM per device.

v0:
```python
import functools
import math

import jax
import jax.numpy as jnp
from jax import lax
from jax.experimental import pallas as pl
from jax.experimental.pallas import tpu as pltpu
from jax.sharding import PartitionSpec as P

HD = 128
TILE = 32
LOW = -1e30
EXP_SCALE = math.log2(math.e) / math.sqrt(HD)
NT = (((1,), (1,)), ((), ()))
NN = (((1,), (0,)), ((), ()))


def sample_bounds(lengths_ref, count):
    starts, ends, total = [], [], jnp.int32(0)
    for j in range(count):
        starts.append(total)
        total = total + lengths_ref[0, j]
        ends.append(total)
    return starts, ends


def stacked_queries(q_ref, tile, g, group):
    first = g * group
    rows = pl.ds(tile * TILE, TILE)
    return jnp.concatenate(
        [q_ref[rows, (first + h) * HD : (first + h + 1) * HD] for h in range(group)], axis=0
    )


def write_heads(out_ref, mixed, total, tile, g, group):
    rows = (mixed * (1.0 / total)).T.astype(out_ref.dtype)
    for h in range(group):
        at = (g * group + h) * HD
        out_ref[pl.ds(tile * TILE, TILE), at : at + HD] = rows[h * TILE : (h + 1) * TILE]


def scores_of(keys, q):
    return lax.dot_general(keys, q, NT, preferred_element_type=jnp.float32)


def absorb(state, scores, values):
    top, total, mixed = state
    new_top = top
    for s in scores:
        new_top = jnp.maximum(new_top, jnp.max(s, axis=0, keepdims=True))
    decay = jnp.exp2((top - new_top) * EXP_SCALE)
    total = total * decay
    mixed = mixed * decay
    for s, v in zip(scores, values):
        w = jnp.exp2((s - new_top) * EXP_SCALE)
        total = total + jnp.sum(w, axis=0, keepdims=True)
        mixed = mixed + lax.dot_general(
            v, w.astype(jnp.bfloat16), NN, preferred_element_type=jnp.float32
        )
    return new_top, total, mixed


def empty(height):
    return (
        jnp.full((1, height), LOW, jnp.float32),
        jnp.zeros((1, height), jnp.float32),
        jnp.zeros((HD, height), jnp.float32),
    )


def row_positions(first, height):
    return first + (lax.broadcasted_iota(jnp.int32, (1, height), 1) & (TILE - 1))


def self_kernel(lengths_ref, place_ref, q_ref, *refs, kv_heads, group, spans, samples):
    pieces, out_ref, stat_ref, mixed_ref = refs[: len(spans)], *refs[len(spans) : len(spans) + 3]
    flipped = refs[len(spans) + 3 :]
    rows_here = q_ref.shape[0]
    height = group * TILE
    base = place_ref[0] * rows_here
    starts, ends = sample_bounds(lengths_ref, samples)

    def lowest_of(t):
        low = jnp.int32(0)
        for e in ends:
            low = jnp.where(e <= t, e, low)
        return low

    def reached(number, low):
        back, count = spans[number]
        piece_end = base - (back - 1) * rows_here
        return (piece_end - count >= 0) & (low < piece_end)

    def flip(number):
        for g in range(kv_heads):
            v = pieces[number][:, (kv_heads + g) * HD : (kv_heads + g + 1) * HD]
            flipped[number][g] = v.T

    flip(0)
    low_here = lowest_of(base)
    for number in range(1, len(spans)):
        pl.when(reached(number, low_here))(functools.partial(flip, number))

    @pl.loop(0, rows_here // TILE)
    def _(tile):
        first = base + tile * TILE
        low = lowest_of(first)
        row_t = row_positions(first, height)
        row_start = jnp.zeros((1, height), jnp.int32)
        for e in ends:
            row_start = jnp.where(e <= row_t, e, row_start)

        def work(number, begin):
            back, count = spans[number]
            piece_start = base - (back - 1) * rows_here - count
            key_t = piece_start + lax.broadcasted_iota(jnp.int32, (count, 1), 0)
            allowed = key_t >= row_start
            if back == 0:
                allowed = allowed & (key_t <= row_t)
            for g in range(kv_heads):
                q = stacked_queries(q_ref, tile, g, group)
                s = scores_of(pieces[number][:, g * HD : (g + 1) * HD], q)
                s = jnp.where(allowed, s, LOW)
                if begin:
                    state = empty(height)
                else:
                    state = stat_ref[g, 0:1, :], stat_ref[g, 1:2, :], mixed_ref[g]
                top, total, mixed = absorb(state, [s], [flipped[number][g]])
                stat_ref[g, 0:1, :] = top
                stat_ref[g, 1:2, :] = total
                mixed_ref[g] = mixed

        work(0, True)
        for number in range(1, len(spans)):
            pl.when(reached(number, low))(functools.partial(work, number, False))
        for g in range(kv_heads):
            write_heads(out_ref, mixed_ref[g], stat_ref[g, 1:2, :], tile, g, group)


def cross_kernel(
    lengths_ref, images_ref, place_ref, q_ref, *refs, kv_heads, group, choices, samples, begin, end
):
    refs = list(refs)
    take = lambda n: [refs.pop(0) for _ in range(n)]
    sources = [take(c) for c in choices]
    stat_in, mixed_in = (None, None) if begin else take(2)
    out_ref = take(1)[0] if end else None
    stat_ref, mixed_ref = take(2)
    keys_ref, flipped_ref = take(2)
    rows_here = q_ref.shape[0]
    height = group * TILE
    base = place_ref[0] * rows_here
    starts, ends = sample_bounds(lengths_ref, samples)
    image_count, _, span, _ = keys_ref.shape

    def lay(ref, at):
        parts, _, each, _ = ref.shape
        for image in range(image_count):
            for g in range(kv_heads):
                k = ref[:, image, :, g * HD : (g + 1) * HD].reshape(parts * each, HD)
                v = ref[:, image, :, (kv_heads + g) * HD : (kv_heads + g + 1) * HD]
                keys_ref[image, g, at : at + parts * each] = k
                flipped_ref[image, g, :, at : at + parts * each] = v.reshape(parts * each, HD).T

    at = 0
    for source in sources:
        if len(source) == 1:
            lay(source[0], at)
        else:
            inner = place_ref[1] == 1
            pl.when(inner)(functools.partial(lay, source[0], at))
            pl.when(jnp.logical_not(inner))(functools.partial(lay, source[1], at))
        at += source[0].shape[0] * source[0].shape[2]

    @pl.loop(0, rows_here // TILE)
    def _(tile):
        slot = 0 if end else tile
        first = base + tile * TILE
        row_t = row_positions(first, height)
        row_image = jnp.zeros((1, height), jnp.int32)
        leading = jnp.int32(0)
        for j in range(samples):
            row_image = jnp.where(row_t >= starts[j], images_ref[0, j], row_image)
            leading = jnp.where(first >= starts[j], images_ref[0, j], leading)

        def work(image, read_stat, read_mixed, at):
            mine = row_image == image
            for g in range(kv_heads):
                q = stacked_queries(q_ref, tile, g, group)
                s = scores_of(keys_ref[image, g], q)
                if read_stat is None:
                    old = empty(height)
                else:
                    old = read_stat[at, g, 0:1, :], read_stat[at, g, 1:2, :], read_mixed[at, g]
                new = absorb(old, [s], [flipped_ref[image, g]])
                top, total, mixed = [jnp.where(mine, n, o) for n, o in zip(new, old)]
                stat_ref[slot, g, 0:1, :] = top
                stat_ref[slot, g, 1:2, :] = total
                mixed_ref[slot, g] = mixed

        work(leading, stat_in, mixed_in, tile)
        for image in range(image_count):
            wanted = jnp.bool_(False)
            for j in range(samples):
                meets = (starts[j] < first + TILE) & (ends[j] > first)
                wanted = wanted | (meets & (images_ref[0, j] == image))
            pl.when(wanted & (leading != image))(
                functools.partial(work, image, stat_ref, mixed_ref, slot)
            )
        if end:
            for g in range(kv_heads):
                write_heads(out_ref, mixed_ref[0, g], stat_ref[0, g, 1:2, :], tile, g, group)


def smem():
    return pl.BlockSpec(memory_space=pltpu.SMEM)


def vmem():
    return pl.BlockSpec(memory_space=pltpu.VMEM)


def cost(rows, width, keys):
    return pl.CostEstimate(
        flops=8 * rows * width * keys, bytes_accessed=4 * rows * width,
        transcendentals=rows * (width // HD) * keys,
    )


def self_attention(lengths, place, q, pieces, spans, kv_heads, group):
    rows, width = q.shape
    height = group * TILE
    return pl.pallas_call(
        functools.partial(
            self_kernel, kv_heads=kv_heads, group=group, spans=spans, samples=lengths.shape[1]
        ),
        out_shape=jax.ShapeDtypeStruct((rows, width), q.dtype),
        in_specs=[smem(), smem(), vmem()] + [vmem() for p in pieces],
        out_specs=vmem(),
        scratch_shapes=[
            pltpu.VMEM((kv_heads, 8, height), jnp.float32),
            pltpu.VMEM((kv_heads, HD, height), jnp.float32),
        ]
        + [pltpu.VMEM((kv_heads, HD, count), q.dtype) for _, count in spans],
        compiler_params=pltpu.CompilerParams(vmem_limit_bytes=24 << 20),
        cost_estimate=cost(rows, width, sum(count for _, count in spans)),
    )(lengths, place, q, *pieces)


def cross_attention(lengths, images, place, q, sources, state, end, kv_heads, group):
    rows, width = q.shape
    height = group * TILE
    begin = state is None
    state = () if begin else state
    tiles = 1 if end else rows // TILE
    stat_shape, mixed_shape = (tiles, kv_heads, 8, height), (tiles, kv_heads, HD, height)
    state_scratch = []
    if end:
        out_shape = jax.ShapeDtypeStruct((rows, width), q.dtype)
        state_scratch = [pltpu.VMEM(s, jnp.float32) for s in (stat_shape, mixed_shape)]
    else:
        out_shape = [jax.ShapeDtypeStruct(s, jnp.float32) for s in (stat_shape, mixed_shape)]
    operands = [piece for source in sources for piece in source]
    image_count = operands[0].shape[1]
    keys = sum(source[0].shape[0] * source[0].shape[2] for source in sources)
    return pl.pallas_call(
        functools.partial(
            cross_kernel, kv_heads=kv_heads, group=group,
            choices=tuple(len(source) for source in sources),
            samples=lengths.shape[1], begin=begin, end=end,
        ),
        out_shape=out_shape,
        in_specs=[smem(), smem(), smem(), vmem()] + [vmem() for p in (*operands, *state)],
        out_specs=vmem() if end else [vmem(), vmem()],
        scratch_shapes=state_scratch
        + [
            pltpu.VMEM((image_count, kv_heads, keys, HD), q.dtype),
            pltpu.VMEM((image_count, kv_heads, HD, keys), q.dtype),
        ],
        compiler_params=pltpu.CompilerParams(vmem_limit_bytes=24 << 20),
        cost_estimate=cost(rows, width, keys),
    )(lengths, images, place, q, *operands, *state)


def per_device(q_self, kv_self, q_cross, kv_cross, sample_lengths, sample_image, *, n_pipe, n_ctx):
    rows = q_self.shape[1]
    kv_heads = kv_self.shape[3] // HD
    group = q_self.shape[2] // HD // kv_heads
    z = lax.axis_index("ctx")
    inner = ((z == 1) | (z == 2)).astype(jnp.int32)
    place = jnp.stack([z, inner]).astype(jnp.int32)

    own = kv_self[0].reshape(rows, -1)
    shift = lambda piece, step: lax.ppermute(
        piece, "ctx", [(c, c + 1) for c in range(step - 1, n_ctx - 1)]
    )
    passed = shift(own, 1)
    arrived = lax.all_to_all(kv_cross, "pipe", split_axis=0, concat_axis=0, tiled=True)
    arrived, passed = lax.optimization_barrier((arrived, passed))
    own_block = arrived.reshape(*arrived.shape[:3], -1)

    longest = rows * n_ctx * 5 // 8
    pieces, spans, left, step = [own, passed], [(0, rows), (1, rows)], longest - 1 - rows, 1
    while left > 0 and step < n_ctx - 1:
        step += 1
        count = min(rows, -(-left // 128) * 128)
        pieces.append(shift(pieces[-1][rows - count :], step))
        spans.append((step, count))
        left -= rows

    self_out = self_attention(
        sample_lengths, place, q_self[0], pieces, tuple(spans), kv_heads, group
    )

    cross = functools.partial(
        cross_attention, sample_lengths, sample_image, place, q_cross[0],
        kv_heads=kv_heads, group=group,
    )
    if n_ctx == 4:
        near = lax.ppermute(own_block, "ctx", [(1, 2), (2, 1)])
        far = lax.ppermute(own_block, "ctx", [(0, 2), (3, 1)])
        pair = lax.ppermute(own_block, "ctx", [(0, 1), (1, 0), (2, 3), (3, 2)])
        near_on = lax.ppermute(near, "ctx", [(1, 0), (2, 3)])
        far_on = lax.ppermute(far, "ctx", [(1, 0), (2, 3)])
        state = cross([[own_block], [pair]], None, False)
        state = cross([[near, near_on]], state, False)
        cross_out = cross([[far, far_on]], state, True)
    else:
        gathered = lax.all_gather(own_block, "ctx", axis=2, tiled=True)
        cross_out = cross([[gathered]], None, True)
    return self_out[None], cross_out[None]


def solution(mesh):
    in_specs = (
        P("pipe", "ctx", "tp"),
        P("pipe", "ctx", None, "tp"),
        P("pipe", "ctx", "tp"),
        P(None, None, ("pipe", "ctx"), None, "tp"),
        P("pipe", None),
        P("pipe", None),
    )
    out_specs = (P("pipe", "ctx", "tp"), P("pipe", "ctx", "tp"))
    body = functools.partial(
        per_device, n_pipe=mesh.shape["pipe"], n_ctx=mesh.shape["ctx"]
    )
    return jax.shard_map(
        body, mesh=mesh, in_specs=in_specs, out_specs=out_specs, check_vma=False
    )
```

profile of v0, /device:TPU:30, one launch (start us, length us, event | category | flops | bytes accessed | tf_op | source)
XLA Modules:
  0.0 97.9 jit_solution(13349718920777028208)
XLA Ops:
  0.6 0.0 copy-start.1
  0.6 0.0 copy-start.3
  0.7 4.3 %all-to-all-start = ((bf16[4,2,64,2,256]{4,3,2,1,0:T(2,128)(2,1)}), bf16[4,2,64,2,256]{4,3,2,1,0:T(2,128)(2,1)S(1)}, u32[]{:S(2)}, u32[]{:S(2)}) async-start(bf16[4,2,64,2,256]{4,3,2,1,0:T(2,128)(2,1)} %param.9), calls=%async_computation | async-start | bytes 1048576 | tf_op jit(solution)/shard_map/all_to_all | solution.py:299
  5.0 1.0 %copy.8 = bf16[32,8,2,256]{3,1,2,0:T(8,128)(2,1)S(1)} copy(bf16[32,8,2,256]{3,2,1,0:T(2,128)(2,1)} %bitcast.16) | data formatting | bytes 524288
  6.0 1.3 %collective-permute-start = (bf16[256,512]{1,0:T(8,128)(2,1)S(1)}, bf16[256,512]{1,0:T(8,128)(2,1)S(1)}, u32[]{:S(2)}, u32[]{:S(2)}) collective-permute-start(bf16[256,512]{1,0:T(8,128)(2,1)S(1)} %bitcast.12), channel_id=1, source_target_pairs={{0,2},{2,4},{4,6},{1,3},{3,5},{5,7},{8,10},{10,12},{12,14},{9,11},... | collective-permute-start | bytes 786440 | tf_op jit(solution)/shard_map/ppermute | solution.py:295
  7.3 8.1 %collective-permute-done.refs_1_ = bf16[256,512]{1,0:T(8,128)(2,1)S(1)} collective-permute-done((bf16[256,512]{1,0:T(8,128)(2,1)S(1)}, bf16[256,512]{1,0:T(8,128)(2,1)S(1)}, u32[]{:S(2)}, u32[]{:S(2)}) %collective-permute-start) | collective-permute-done | bytes 262176 | tf_op jit(solution)/shard_map/ppermute | solution.py:295
  15.4 0.0 all-to-all-done
  15.4 0.3 reshape.7.refs_0_
  15.7 0.7 collective-permute-start.5
  16.4 5.1 %collective-permute-start.3 = (bf16[4,2,64,512]{3,2,1,0:T(8,128)(2,1)S(1)}, bf16[4,2,64,512]{3,2,1,0:T(8,128)(2,1)S(1)}, u32[]{:S(2)}, u32[]{:S(2)}) collective-permute-start(bf16[4,2,64,512]{3,2,1,0:T(8,128)(2,1)S(1)} %reshape.7.refs_0_), channel_id=1, source_target_pairs={{0,4},{6,2},{1,5},{7,3},{8,12},{14,10},{9,13},{15,11},{16,20},{22,... | collective-permute-start | bytes 1572872 | tf_op jit(solution)/shard_map/ppermute | solution.py:322
  21.5 1.3 %collective-permute-start.1 = (bf16[256,512]{1,0:T(8,128)(2,1)S(1)}, bf16[256,512]{1,0:T(8,128)(2,1)S(1)}, u32[]{:S(2)}, u32[]{:S(2)}) collective-permute-start(bf16[256,512]{1,0:T(8,128)(2,1)S(1)} %collective-permute-done.refs_1_), channel_id=1, source_target_pairs={{2,4},{4,6},{3,5},{5,7},{10,12},{12,14},{11,13},{13,15},{18,20},{2... | collective-permute-start | bytes 786440 | tf_op jit(solution)/shard_map/ppermute | solution.py:295
  22.8 2.7 %collective-permute-start.7 = (bf16[4,2,64,512]{3,2,1,0:T(8,128)(2,1)S(1)}, bf16[4,2,64,512]{3,2,1,0:T(8,128)(2,1)}, u32[]{:S(2)}, u32[]{:S(2)}) collective-permute-start(bf16[4,2,64,512]{3,2,1,0:T(8,128)(2,1)S(1)} %reshape.7.refs_0_), channel_id=1, source_target_pairs={{0,2},{2,0},{4,6},{6,4},{1,3},{3,1},{5,7},{7,5},{8,10},{10,8},{12,... | collective-permute-start | bytes 1572872 | tf_op jit(solution)/shard_map/ppermute | solution.py:323
  25.5 7.1 %collective-permute-done.1.refs_2_ = bf16[256,512]{1,0:T(8,128)(2,1)S(1)} collective-permute-done((bf16[256,512]{1,0:T(8,128)(2,1)S(1)}, bf16[256,512]{1,0:T(8,128)(2,1)S(1)}, u32[]{:S(2)}, u32[]{:S(2)}) %collective-permute-start.1) | collective-permute-done | bytes 262176 | tf_op jit(solution)/shard_map/ppermute | solution.py:295
  32.6 0.7 slice.4
  33.3 1.3 %collective-permute-start.2 = (bf16[128,512]{1,0:T(8,128)(2,1)}, bf16[128,512]{1,0:T(8,128)(2,1)S(1)}, u32[]{:S(2)}, u32[]{:S(2)}) collective-permute-start(bf16[128,512]{1,0:T(8,128)(2,1)} %slice.4), channel_id=1, source_target_pairs={{4,6},{5,7},{12,14},{13,15},{20,22},{21,23},{28,30},{29,31}} | collective-permute-start | bytes 393224 | tf_op jit(solution)/shard_map/ppermute | solution.py:295
  34.6 0.1 pad_add_fusion.place_ref
  34.6 0.0 collective-permute-done.5.refs_0_
  34.6 1.3 %collective-permute-start.6 = (bf16[4,2,64,512]{3,2,1,0:T(8,128)(2,1)S(1)}, bf16[4,2,64,512]{3,2,1,0:T(8,128)(2,1)S(1)}, u32[]{:S(2)}, u32[]{:S(2)}) collective-permute-start(bf16[4,2,64,512]{3,2,1,0:T(8,128)(2,1)S(1)} %collective-permute-done.5.refs_0_), channel_id=1, source_target_pairs={{2,0},{4,6},{3,1},{5,7},{10,8},{12,14},{11,9},{13,15},{18,16},{20,... | collective-permute-start | bytes 1572872 | tf_op jit(solution)/shard_map/ppermute | solution.py:324
  35.9 0.0 collective-permute-done.3.refs_0_
  35.9 1.3 %collective-permute-start.4 = (bf16[4,2,64,512]{3,2,1,0:T(8,128)(2,1)S(1)}, bf16[4,2,64,512]{3,2,1,0:T(8,128)(2,1)S(1)}, u32[]{:S(2)}, u32[]{:S(2)}) collective-permute-start(bf16[4,2,64,512]{3,2,1,0:T(8,128)(2,1)S(1)} %collective-permute-done.3.refs_0_), channel_id=1, source_target_pairs={{2,0},{4,6},{3,1},{5,7},{10,8},{12,14},{11,9},{13,15},{18,16},{20,... | collective-permute-start | bytes 1572872 | tf_op jit(solution)/shard_map/ppermute | solution.py:325
  37.2 16.4 %collective-permute-done.2.refs_3_ = bf16[128,512]{1,0:T(8,128)(2,1)S(1)} collective-permute-done((bf16[128,512]{1,0:T(8,128)(2,1)}, bf16[128,512]{1,0:T(8,128)(2,1)S(1)}, u32[]{:S(2)}, u32[]{:S(2)}) %collective-permute-start.2) | collective-permute-done | bytes 131104 | tf_op jit(solution)/shard_map/ppermute | solution.py:295
  53.6 0.0 copy-done.1
  53.6 0.0 copy-done.3
  53.6 0.0 copy-start
  53.6 0.0 copy-start.2
  53.6 19.8 %shard_map.77 = bf16[256,2048]{1,0:T(8,128)(2,1)} custom-call(s32[1,8]{1,0:T(1,128)S(1)} %copy-done.1, s32[2]{0:T(128)S(1)} %pad_add_fusion.place_ref, bf16[256,2048]{1,0:T(8,128)(2,1)S(1)} %bitcast.14, bf16[256,512]{1,0:T(8,128)(2,1)S(1)} %bitcast.13, bf16[256,512]{1,0:T(8,128)(2,1)S(1)} %collective-permute-done.refs_1_, ...), custom_call_target="tpu_custom_call" | custom-call | flops 3758096384 | bytes 2097152 | tf_op jit(solution)/shard_map/pallas_call | solution.py:234
  73.5 0.0 collective-permute-done.7.refs_1_
  73.5 0.0 copy-done
  73.5 0.0 copy-done.2
  73.5 9.4 %shard_map.78 = (f32[8,2,8,256]{3,2,1,0:T(8,128)S(1)}, f32[8,2,128,256]{3,2,1,0:T(8,128)S(1)}) custom-call(s32[1,8]{1,0:T(1,128)S(1)} %copy-done.1, s32[1,8]{1,0:T(1,128)S(1)} %copy-done.2, s32[2]{0:T(128)S(1)} %pad_add_fusion.place_ref, bf16[256,2048]{1,0:T(8,128)(2,1)S(1)} %bitcast.9, bf16[4,2,64,512]{3,2,1,0:T(8,128)(2,1)S(1)} %reshape.7.refs_0_, ...), custom_call_target="tpu_custom_call" | custom-call | flops 2147483648 | bytes 2097152 | tf_op jit(solution)/shard_map/pallas_call | solution.py:267
  82.9 0.0 collective-permute-done.6.refs_1_
  82.9 6.6 %shard_map.79 = (f32[8,2,8,256]{3,2,1,0:T(8,128)S(1)}, f32[8,2,128,256]{3,2,1,0:T(8,128)S(1)}) custom-call(s32[1,8]{1,0:T(1,128)S(1)} %copy-done.1, s32[1,8]{1,0:T(1,128)S(1)} %copy-done.2, s32[2]{0:T(128)S(1)} %pad_add_fusion.place_ref, bf16[256,2048]{1,0:T(8,128)(2,1)S(1)} %bitcast.10, bf16[4,2,64,512]{3,2,1,0:T(8,128)(2,1)S(1)} %collective-permute-done.5.refs_0_, ...), custom_call_target="tpu_custom_call" | custom-call | flops 1073741824 | bytes 2097152 | tf_op jit(solution)/shard_map/pallas_call | solution.py:267
  89.5 0.0 collective-permute-done.4.refs_1_
  89.5 8.4 %shard_map.80 = bf16[256,2048]{1,0:T(8,128)(2,1)} custom-call(s32[1,8]{1,0:T(1,128)S(1)} %copy-done.1, s32[1,8]{1,0:T(1,128)S(1)} %copy-done.2, s32[2]{0:T(128)S(1)} %pad_add_fusion.place_ref, bf16[256,2048]{1,0:T(8,128)(2,1)S(1)} %bitcast.11, bf16[4,2,64,512]{3,2,1,0:T(8,128)(2,1)S(1)} %collective-permute-done.3.refs_0_, ...), custom_call_target="tpu_custom_call" | custom-call | flops 1073741824 | bytes 2097152 | tf_op jit(solution)/shard_map/pallas_call | solution.py:267
Async XLA Ops:
  0.6 53.0 %copy-start.1 = (s32[1,8]{1,0:T(1,128)S(1)}, s32[1,8]{1,0:T(1,128)}, u32[]{:S(2)}) copy-start(s32[1,8]{1,0:T(1,128)} %lengths_ref.7) | copy-start | bytes 100
  0.6 53.0 %copy-start.3 = (bf16[1,256,2048]{2,1,0:T(8,128)(2,1)S(1)}, bf16[1,256,2048]{2,1,0:T(8,128)(2,1)}, u32[]{:S(2)}) copy-start(bf16[1,256,2048]{2,1,0:T(8,128)(2,1)} %param.6) | copy-start | bytes 3145732
  0.7 14.7 %all-to-all-start = ((bf16[4,2,64,2,256]{4,3,2,1,0:T(2,128)(2,1)}), bf16[4,2,64,2,256]{4,3,2,1,0:T(2,128)(2,1)S(1)}, u32[]{:S(2)}, u32[]{:S(2)}) async-start(bf16[4,2,64,2,256]{4,3,2,1,0:T(2,128)(2,1)} %param.9), calls=%async_computation | async-start | bytes 1048576 | tf_op jit(solution)/shard_map/all_to_all | solution.py:299
  6.0 9.4 %collective-permute-start = (bf16[256,512]{1,0:T(8,128)(2,1)S(1)}, bf16[256,512]{1,0:T(8,128)(2,1)S(1)}, u32[]{:S(2)}, u32[]{:S(2)}) collective-permute-start(bf16[256,512]{1,0:T(8,128)(2,1)S(1)} %bitcast.12), channel_id=1, source_target_pairs={{0,2},{2,4},{4,6},{1,3},{3,5},{5,7},{8,10},{10,12},{12,14},{9,11},... | collective-permute-start | bytes 786440 | tf_op jit(solution)/shard_map/ppermute | solution.py:295
  15.7 19.0 %collective-permute-start.5 = (bf16[4,2,64,512]{3,2,1,0:T(8,128)(2,1)S(1)}, bf16[4,2,64,512]{3,2,1,0:T(8,128)(2,1)S(1)}, u32[]{:S(2)}, u32[]{:S(2)}) collective-permute-start(bf16[4,2,64,512]{3,2,1,0:T(8,128)(2,1)S(1)} %reshape.7.refs_0_), channel_id=1, source_target_pairs={{2,4},{4,2},{3,5},{5,3},{10,12},{12,10},{11,13},{13,11},{18,20},{2... | collective-permute-start | bytes 1572872 | tf_op jit(solution)/shard_map/ppermute | solution.py:321
  16.4 19.5 %collective-permute-start.3 = (bf16[4,2,64,512]{3,2,1,0:T(8,128)(2,1)S(1)}, bf16[4,2,64,512]{3,2,1,0:T(8,128)(2,1)S(1)}, u32[]{:S(2)}, u32[]{:S(2)}) collective-permute-start(bf16[4,2,64,512]{3,2,1,0:T(8,128)(2,1)S(1)} %reshape.7.refs_0_), channel_id=1, source_target_pairs={{0,4},{6,2},{1,5},{7,3},{8,12},{14,10},{9,13},{15,11},{16,20},{22,... | collective-permute-start | bytes 1572872 | tf_op jit(solution)/shard_map/ppermute | solution.py:322
  21.5 11.1 %collective-permute-start.1 = (bf16[256,512]{1,0:T(8,128)(2,1)S(1)}, bf16[256,512]{1,0:T(8,128)(2,1)S(1)}, u32[]{:S(2)}, u32[]{:S(2)}) collective-permute-start(bf16[256,512]{1,0:T(8,128)(2,1)S(1)} %collective-permute-done.refs_1_), channel_id=1, source_target_pairs={{2,4},{4,6},{3,5},{5,7},{10,12},{12,14},{11,13},{13,15},{18,20},{2... | collective-permute-start | bytes 786440 | tf_op jit(solution)/shard_map/ppermute | solution.py:295
  22.8 50.7 %collective-permute-start.7 = (bf16[4,2,64,512]{3,2,1,0:T(8,128)(2,1)S(1)}, bf16[4,2,64,512]{3,2,1,0:T(8,128)(2,1)}, u32[]{:S(2)}, u32[]{:S(2)}) collective-permute-start(bf16[4,2,64,512]{3,2,1,0:T(8,128)(2,1)S(1)} %reshape.7.refs_0_), channel_id=1, source_target_pairs={{0,2},{2,0},{4,6},{6,4},{1,3},{3,1},{5,7},{7,5},{8,10},{10,8},{12,... | collective-permute-start | bytes 1572872 | tf_op jit(solution)/shard_map/ppermute | solution.py:323
  33.3 20.4 %collective-permute-start.2 = (bf16[128,512]{1,0:T(8,128)(2,1)}, bf16[128,512]{1,0:T(8,128)(2,1)S(1)}, u32[]{:S(2)}, u32[]{:S(2)}) collective-permute-start(bf16[128,512]{1,0:T(8,128)(2,1)} %slice.4), channel_id=1, source_target_pairs={{4,6},{5,7},{12,14},{13,15},{20,22},{21,23},{28,30},{29,31}} | collective-permute-start | bytes 393224 | tf_op jit(solution)/shard_map/ppermute | solution.py:295
  34.6 48.2 %collective-permute-start.6 = (bf16[4,2,64,512]{3,2,1,0:T(8,128)(2,1)S(1)}, bf16[4,2,64,512]{3,2,1,0:T(8,128)(2,1)S(1)}, u32[]{:S(2)}, u32[]{:S(2)}) collective-permute-start(bf16[4,2,64,512]{3,2,1,0:T(8,128)(2,1)S(1)} %collective-permute-done.5.refs_0_), channel_id=1, source_target_pairs={{2,0},{4,6},{3,1},{5,7},{10,8},{12,14},{11,9},{13,15},{18,16},{20,... | collective-permute-start | bytes 1572872 | tf_op jit(solution)/shard_map/ppermute | solution.py:324
  35.9 53.6 %collective-permute-start.4 = (bf16[4,2,64,512]{3,2,1,0:T(8,128)(2,1)S(1)}, bf16[4,2,64,512]{3,2,1,0:T(8,128)(2,1)S(1)}, u32[]{:S(2)}, u32[]{:S(2)}) collective-permute-start(bf16[4,2,64,512]{3,2,1,0:T(8,128)(2,1)S(1)} %collective-permute-done.3.refs_0_), channel_id=1, source_target_pairs={{2,0},{4,6},{3,1},{5,7},{10,8},{12,14},{11,9},{13,15},{18,16},{20,... | collective-permute-start | bytes 1572872 | tf_op jit(solution)/shard_map/ppermute | solution.py:325
  53.6 19.8 %copy-start = (bf16[1,256,2048]{2,1,0:T(8,128)(2,1)S(1)}, bf16[1,256,2048]{2,1,0:T(8,128)(2,1)}, u32[]{:S(2)}) copy-start(bf16[1,256,2048]{2,1,0:T(8,128)(2,1)} %param.8) | copy-start | bytes 3145732
  53.6 19.8 %copy-start.2 = (s32[1,8]{1,0:T(1,128)S(1)}, s32[1,8]{1,0:T(1,128)}, u32[]{:S(2)}) copy-start(s32[1,8]{1,0:T(1,128)} %images_ref.5) | copy-start | bytes 100
where the time goes:
time: 99.6 us; the launch traced here: 97.9 us
  Pallas kernels  44.2 us (44%)
  waiting for transfers between devices  31.6 us (32%)
  starting transfers between devices  19.2 us (19%)
  local copies, waits for them, and re-layouts  1.99 us (2%)
    ppermute x3, waiting for transfers between devices, per_device(): lax.ppermute(piece, 'ctx', [(c, c + 1) for c in range(step - 1, n_ctx - 1)])  31.6 us
    pallas_call x3, Pallas kernels, cross_attention(): pl.pallas_call(functools.partial(cross_kernel, kv_heads=kv_heads, group=g...  24.4 us
    pallas_call x1, Pallas kernels, self_attention(): pl.pallas_call(functools.partial(self_kernel, kv_heads=kv_heads, group=gr...  19.8 us
    ppermute x1, starting transfers between devices, per_device(): far = lax.ppermute(own_block, 'ctx', [(0, 2), (3, 1)])  5.06 us
    all_to_all x1, starting transfers between devices, per_device(): lax.all_to_all(kv_cross, 'pipe', split_axis=0, concat_axis=0, tiled=True)  4.34 us
    ppermute x3, starting transfers between devices, per_device(): lax.ppermute(piece, 'ctx', [(c, c + 1) for c in range(step - 1, n_ctx - 1)])  3.86 us
    ppermute x1, starting transfers between devices, per_device(): pair = lax.ppermute(own_block, 'ctx', [(0, 1), (1, 0), (2, 3), (3, 2)])  2.71 us
  transfers between devices with their start and end apart: 9, of which 3 were waited for; matrix products, arithmetic and copies ran while one was open for 2% of the time, Pallas kernels for 37%

commit v1 on v0

v1 whole, which is shorter than its diff:
```python
import functools
import math

import jax
import jax.numpy as jnp
from jax import lax
from jax.experimental import pallas as pl
from jax.experimental.pallas import tpu as pltpu
from jax.sharding import PartitionSpec as P

HD = 128
TILE = 32
TOGETHER = 4
LOW = -1e30
EXP_SCALE = math.log2(math.e) / math.sqrt(HD)
NT = (((1,), (1,)), ((), ()))
NN = (((1,), (0,)), ((), ()))


def sample_bounds(lengths_ref, count):
    starts, ends, total = [], [], jnp.int32(0)
    for j in range(count):
        starts.append(total)
        total = total + lengths_ref[0, j]
        ends.append(total)
    return starts, ends


def stacked_queries(q_ref, tile, g, group):
    first = g * group
    rows = pl.ds(tile * TILE, TILE)
    return jnp.concatenate(
        [q_ref[rows, (first + h) * HD : (first + h + 1) * HD] for h in range(group)], axis=0
    )


def write_heads(out_ref, mixed, total, tile, g, group):
    rows = (mixed * (1.0 / total)).T.astype(out_ref.dtype)
    for h in range(group):
        at = (g * group + h) * HD
        out_ref[pl.ds(tile * TILE, TILE), at : at + HD] = rows[h * TILE : (h + 1) * TILE]


def scores_of(keys, q):
    return lax.dot_general(keys, q, NT, preferred_element_type=jnp.float32)


def absorb(state, s, v):
    if state is None:
        new_top = jnp.max(s, axis=0, keepdims=True)
    else:
        top, total, mixed = state
        new_top = jnp.maximum(top, jnp.max(s, axis=0, keepdims=True))
    w = jnp.exp2((s - new_top) * EXP_SCALE)
    added = jnp.sum(w, axis=0, keepdims=True)
    product = lax.dot_general(v, w.astype(jnp.bfloat16), NN, preferred_element_type=jnp.float32)
    if state is None:
        return new_top, added, product
    decay = jnp.exp2((top - new_top) * EXP_SCALE)
    return new_top, total * decay + added, mixed * decay + product


def staggered(units, score, finish):
    waiting = None
    for unit in units:
        s = score(*unit)
        if waiting is not None:
            finish(*waiting)
        waiting = (*unit, s)
    finish(*waiting)


def row_positions(first, height):
    return first + (lax.broadcasted_iota(jnp.int32, (1, height), 1) & (TILE - 1))


def lay(keys_at, flipped_at, ref, rows, kv_heads, g):
    keys_at[...] = ref[rows, g * HD : (g + 1) * HD]
    flipped_at[...] = ref[rows, (kv_heads + g) * HD : (kv_heads + g + 1) * HD].T


def self_kernel(lengths_ref, place_ref, q_ref, *refs, kv_heads, group, spans, parts, samples):
    sources = {part[1] for part in parts}
    pieces = refs[: len(sources)]
    out_ref, stat_ref, mixed_ref, keys_ref, flipped_ref = refs[len(sources) :]
    rows_here = q_ref.shape[0]
    tiles = rows_here // TILE
    height = group * TILE
    base = place_ref[0] * rows_here
    _, ends = sample_bounds(lengths_ref, samples)
    ats = [sum(count for _, count in spans[:n]) for n in range(len(spans))]

    lows = []
    for tile in range(tiles):
        low = jnp.int32(0)
        for e in ends:
            low = jnp.where(e <= base + tile * TILE, e, low)
        lows.append(low)

    def limits(number):
        back, count = spans[number]
        end = base - (back - 1) * rows_here
        return end - count, end

    def reached(number):
        start, end = limits(number)
        many = jnp.int32(0)
        for low in lows:
            many = many + (low < end).astype(jnp.int32)
        return jnp.where(start >= 0, many, 0)

    counts = [reached(number) for number in range(1, len(spans))]
    for number, source, at, offset, count, only in parts:

        def fill(number=number, source=source, at=at, offset=offset, count=count):
            here = slice(ats[number] + offset, ats[number] + offset + count)
            for g in range(kv_heads):
                lay(
                    keys_ref.at[g, here], flipped_ref.at[g, :, here], pieces[source],
                    slice(at, at + count), kv_heads, g,
                )

        if number == 0:
            fill()
        else:
            asked = counts[number - 1] > 0
            if only is not None:
                asked = asked & (place_ref[0] == only)
            pl.when(asked)(fill)

    def starts_of(first):
        row_t = row_positions(first, height)
        row_start = jnp.zeros((1, height), jnp.int32)
        for e in ends:
            row_start = jnp.where(e <= row_t, e, row_start)
        return row_start, row_t

    def keep(tile, g, state):
        stat_ref[tile, g, 0:1, :] = state[0]
        stat_ref[tile, g, 1:2, :] = state[1]
        mixed_ref[tile, g] = state[2]

    def own_count(tile):
        return min(rows_here, -(-(tile + 1) * TILE // HD) * HD)

    def own_scores(tile, g):
        q = stacked_queries(q_ref, tile, g, group)
        return scores_of(keys_ref[g, : own_count(tile)], q)

    def own_finish(tile, g, s):
        row_start, row_t = starts_of(base + tile * TILE)
        key_t = base + lax.broadcasted_iota(jnp.int32, (own_count(tile), 1), 0)
        s = jnp.where((key_t >= row_start) & (key_t <= row_t), s, LOW)
        keep(tile, g, absorb(None, s, flipped_ref[g, :, : own_count(tile)]))

    staggered(
        [(tile, g) for tile in range(tiles) for g in range(kv_heads)], own_scores, own_finish
    )

    together = math.gcd(tiles, TOGETHER)
    for number in range(1, len(spans)):
        start, _ = limits(number)
        at, count = ats[number], spans[number][1]

        @pl.loop(0, (counts[number - 1] + together - 1) // together)
        def _(turn, start=start, at=at, count=count):
            def scores(n, g):
                q = stacked_queries(q_ref, turn * together + n, g, group)
                return scores_of(keys_ref[g, at : at + count], q)

            def finish(n, g, s):
                tile = turn * together + n
                row_start, _ = starts_of(base + tile * TILE)
                key_t = start + lax.broadcasted_iota(jnp.int32, (count, 1), 0)
                s = jnp.where(key_t >= row_start, s, LOW)
                old = stat_ref[tile, g, 0:1, :], stat_ref[tile, g, 1:2, :], mixed_ref[tile, g]
                keep(tile, g, absorb(old, s, flipped_ref[g, :, at : at + count]))

            staggered(
                [(n, g) for n in range(together) for g in range(kv_heads)], scores, finish
            )

    for tile in range(tiles):
        for g in range(kv_heads):
            write_heads(out_ref, mixed_ref[tile, g], stat_ref[tile, g, 1:2, :], tile, g, group)


def cross_kernel(
    lengths_ref, images_ref, place_ref, q_ref, *refs, kv_heads, group, sources, samples, begin, end
):
    refs = list(refs)
    take = lambda n: [refs.pop(0) for _ in range(n)]
    pieces = [take(len(source)) for source in sources]
    stat_in, mixed_in = (None, None) if begin else take(2)
    out_ref = take(1)[0] if end else None
    stat_ref, mixed_ref, keys_ref, flipped_ref = take(4)
    rows_here = q_ref.shape[0]
    tiles = rows_here // TILE
    height = group * TILE
    base = place_ref[0] * rows_here
    starts, _ = sample_bounds(lengths_ref, samples)
    image_count = keys_ref.shape[0]

    def fill(ref, at, row, parts, each):
        for part in range(parts):
            for image in range(image_count):
                rows = slice(row + (part * image_count + image) * each, None)
                rows = slice(rows.start, rows.start + each)
                here = slice(at + part * each, at + (part + 1) * each)
                for g in range(kv_heads):
                    keys_ref[image, g, here] = ref[rows, g * HD : (g + 1) * HD]
        for image in range(image_count):
            for g in range(kv_heads):
                column = (kv_heads + g) * HD
                values = [
                    ref[pl.ds(row + (part * image_count + image) * each, each), column : column + HD]
                    for part in range(parts)
                ]
                whole = jnp.concatenate(values, axis=0)
                flipped_ref[image, g, :, at : at + parts * each] = whole.T

    at = 0
    for source, given in zip(sources, pieces):
        for number, ((row, parts, each), ref) in enumerate(zip(source, given)):
            put = functools.partial(fill, ref, at, row, parts, each)
            if len(source) == 1:
                put()
            else:
                pl.when(place_ref[1] == 1 - number)(put)
        at += source[0][1] * source[0][2]

    def images_of(tile):
        first = base + tile * TILE
        row_t = row_positions(first, height)
        row_image = jnp.zeros((1, height), jnp.int32)
        leading = jnp.int32(0)
        for j in range(samples):
            row_image = jnp.where(row_t >= starts[j], images_ref[0, j], row_image)
            leading = jnp.where(first >= starts[j], images_ref[0, j], leading)
        return row_image, leading

    def keep(tile, g, state):
        stat_ref[tile, g, 0:1, :] = state[0]
        stat_ref[tile, g, 1:2, :] = state[1]
        mixed_ref[tile, g] = state[2]

    def chosen(mine, new, old):
        if old is None:
            old = LOW, 0.0, 0.0
        return [jnp.where(mine, n, o) for n, o in zip(new, old)]

    marks = [images_of(tile) for tile in range(tiles)]

    def scores(tile, g):
        return scores_of(keys_ref[marks[tile][1], g], stacked_queries(q_ref, tile, g, group))

    def finish(tile, g, s):
        row_image, leading = marks[tile]
        old = None
        if not begin:
            old = stat_in[tile, g, 0:1, :], stat_in[tile, g, 1:2, :], mixed_in[tile, g]
        new = absorb(old, s, flipped_ref[leading, g])
        keep(tile, g, chosen(row_image == leading, new, old))

    staggered([(tile, g) for tile in range(tiles) for g in range(kv_heads)], scores, finish)

    @pl.loop(0, tiles)
    def _(tile):
        first = base + tile * TILE
        leading, others = jnp.int32(0), [jnp.bool_(False)] * image_count
        for j in range(samples):
            leading = jnp.where(first >= starts[j], images_ref[0, j], leading)
        for j in range(samples):
            inside = (starts[j] > first) & (starts[j] < first + TILE)
            for image in range(image_count):
                others[image] = others[image] | (inside & (images_ref[0, j] == image))
        for image in range(image_count):

            @pl.when(others[image] & (leading != image))
            def _(image=image):
                row_image, _ = images_of(tile)
                olds = [
                    (stat_ref[tile, g, 0:1, :], stat_ref[tile, g, 1:2, :], mixed_ref[tile, g])
                    for g in range(kv_heads)
                ]
                ss = [
                    scores_of(keys_ref[image, g], stacked_queries(q_ref, tile, g, group))
                    for g in range(kv_heads)
                ]
                for g in range(kv_heads):
                    new = absorb(olds[g], ss[g], flipped_ref[image, g])
                    keep(tile, g, chosen(row_image == image, new, olds[g]))

    if end:
        for tile in range(tiles):
            for g in range(kv_heads):
                write_heads(out_ref, mixed_ref[tile, g], stat_ref[tile, g, 1:2, :], tile, g, group)


def smem():
    return pl.BlockSpec(memory_space=pltpu.SMEM)


def vmem():
    return pl.BlockSpec(memory_space=pltpu.VMEM)


def cost(rows, width, keys):
    return pl.CostEstimate(
        flops=8 * rows * width * keys, bytes_accessed=4 * rows * width,
        transcendentals=rows * (width // HD) * keys,
    )


def state_shapes(rows, kv_heads, group):
    tiles, height = rows // TILE, group * TILE
    return (tiles, kv_heads, 8, height), (tiles, kv_heads, HD, height)


def self_attention(lengths, place, q, pieces, spans, parts, kv_heads, group):
    rows, width = q.shape
    keys = sum(count for _, count in spans)
    return pl.pallas_call(
        functools.partial(
            self_kernel, kv_heads=kv_heads, group=group, spans=spans, parts=parts,
            samples=lengths.shape[1],
        ),
        out_shape=jax.ShapeDtypeStruct((rows, width), q.dtype),
        in_specs=[smem(), smem(), vmem()] + [vmem() for p in pieces],
        out_specs=vmem(),
        scratch_shapes=[pltpu.VMEM(s, jnp.float32) for s in state_shapes(rows, kv_heads, group)]
        + [
            pltpu.VMEM((kv_heads, keys, HD), q.dtype),
            pltpu.VMEM((kv_heads, HD, keys), q.dtype),
        ],
        compiler_params=pltpu.CompilerParams(vmem_limit_bytes=28 << 20),
        cost_estimate=cost(rows, width, keys),
    )(lengths, place, q, *pieces)


def cross_attention(lengths, images, place, q, sources, state, end, kv_heads, group, image_count):
    rows, width = q.shape
    begin = state is None
    state = () if begin else state
    shapes = state_shapes(rows, kv_heads, group)
    state_scratch = []
    if end:
        out_shape = jax.ShapeDtypeStruct((rows, width), q.dtype)
        state_scratch = [pltpu.VMEM(s, jnp.float32) for s in shapes]
    else:
        out_shape = [jax.ShapeDtypeStruct(s, jnp.float32) for s in shapes]
    operands = [piece[0] for source in sources for piece in source]
    keys = sum(source[0][2] * source[0][3] for source in sources)
    return pl.pallas_call(
        functools.partial(
            cross_kernel, kv_heads=kv_heads, group=group,
            sources=tuple(tuple(piece[1:] for piece in source) for source in sources),
            samples=lengths.shape[1], begin=begin, end=end,
        ),
        out_shape=out_shape,
        in_specs=[smem(), smem(), smem(), vmem()] + [vmem() for p in (*operands, *state)],
        out_specs=vmem() if end else [vmem(), vmem()],
        scratch_shapes=state_scratch
        + [
            pltpu.VMEM((image_count, kv_heads, keys, HD), q.dtype),
            pltpu.VMEM((image_count, kv_heads, HD, keys), q.dtype),
        ],
        compiler_params=pltpu.CompilerParams(vmem_limit_bytes=28 << 20),
        cost_estimate=cost(rows, width, keys),
    )(lengths, images, place, q, *operands, *state)


def per_device(q_self, kv_self, q_cross, kv_cross, sample_lengths, sample_image, *, n_pipe, n_ctx):
    rows = q_self.shape[1]
    kv_heads = kv_self.shape[3] // HD
    group = q_self.shape[2] // HD // kv_heads
    image_count, each = kv_cross.shape[1:3]
    z = lax.axis_index("ctx")
    inner = ((z == 1) | (z == 2)).astype(jnp.int32)
    place = jnp.stack([z, inner]).astype(jnp.int32)

    own = kv_self[0].reshape(rows, -1)
    shift = lambda piece, step: lax.ppermute(
        piece, "ctx", [(c, c + 1) for c in range(step - 1, n_ctx - 1)]
    )
    passed = shift(own, 1)
    arrived = lax.all_to_all(kv_cross, "pipe", split_axis=0, concat_axis=0, tiled=True)
    arrived, passed = lax.optimization_barrier((arrived, passed))
    own_rows = arrived.reshape(-1, own.shape[1])
    cross_rows = own_rows.shape[0]
    longest = rows * n_ctx * 5 // 8

    attend_self = functools.partial(
        self_attention, sample_lengths, place, q_self[0], kv_heads=kv_heads, group=group
    )
    attend_cross = functools.partial(
        cross_attention, sample_lengths, sample_image, place, q_cross[0],
        kv_heads=kv_heads, group=group, image_count=image_count,
    )
    if n_ctx == 4:
        half = rows // 2
        block = jnp.concatenate([passed[half:], own_rows, passed[:half]], axis=0)
        at = lambda array, row: (array, row, n_pipe, each)
        near = lax.ppermute(block, "ctx", [(1, 2), (2, 1)])
        pair = lax.ppermute(block, "ctx", [(0, 1), (1, 0), (2, 3), (3, 2)])
        state = attend_cross([[at(own_rows, 0)]], None, False)
        near, pair, state = lax.optimization_barrier((near, pair, state))
        far = lax.ppermute(pair[half : half + cross_rows], "ctx", [(1, 2), (2, 1)])
        near_on = lax.ppermute(near[: half + cross_rows], "ctx", [(1, 0), (2, 3)])
        state = attend_cross([[at(pair, half)]], state, False)
        far, near_on, state = lax.optimization_barrier((far, near_on, state))
        far_on = lax.ppermute(far, "ctx", [(1, 0), (2, 3)])
        state = attend_cross([[at(near, half), at(near_on, half)]], state, False)
        low = half + cross_rows
        spans = ((0, rows), (1, rows), (2, rows), (3, half))
        parts = (
            (0, 0, 0, 0, rows, None),
            (1, 1, 0, 0, rows, None),
            (2, 2, low, 0, half, 2),
            (2, 2, 0, half, half, 2),
            (2, 3, low, 0, half, 3),
            (2, 3, 0, half, half, 3),
            (3, 4, 0, 0, half, 3),
        )
        self_out = attend_self([own, passed, near, pair, near_on], spans, parts)
        cross_out = attend_cross([[at(far, 0), at(far_on, 0)]], state, True)
    else:
        pieces, spans, left, step = [own, passed], [(0, rows), (1, rows)], longest - 1 - rows, 1
        while left > 0 and step < n_ctx - 1:
            step += 1
            count = min(rows, -(-left // HD) * HD)
            pieces.append(shift(pieces[-1][rows - count :], step))
            spans.append((step, count))
            left -= rows
        parts = tuple((n, n, 0, 0, count, None) for n, (_, count) in enumerate(spans))
        self_out = attend_self(pieces, tuple(spans), parts)
        gathered = lax.all_gather(own_rows, "ctx", axis=0, tiled=True)
        cross_out = attend_cross([[(gathered, 0, n_ctx * n_pipe, each)]], None, True)
    return self_out[None], cross_out[None]


def solution(mesh):
    in_specs = (
        P("pipe", "ctx", "tp"),
        P("pipe", "ctx", None, "tp"),
        P("pipe", "ctx", "tp"),
        P(None, None, ("pipe", "ctx"), None, "tp"),
        P("pipe", None),
        P("pipe", None),
    )
    out_specs = (P("pipe", "ctx", "tp"), P("pipe", "ctx", "tp"))
    body = functools.partial(
        per_device, n_pipe=mesh.shape["pipe"], n_ctx=mesh.shape["ctx"]
    )
    return jax.shard_map(
        body, mesh=mesh, in_specs=in_specs, out_specs=out_specs, check_vma=False
    )
```

time: 99.6 us -> 74.6 us (0.75)
  the two profiles are of different devices: /device:TPU:30 before, /device:TPU:0 now
where the time goes in v1:
time: 74.6 us; the launch traced here: 74.2 us
  waiting for transfers between devices  29.3 us (39%)
  Pallas kernels  26.6 us (36%)
  starting transfers between devices  15.3 us (21%)
  local copies, waits for them, and re-layouts  1.19 us (2%)
  other arithmetic  1.01 us (1%)
  between operations  0.78 us (1%)
    pallas_call x4, Pallas kernels, cross_attention(): pl.pallas_call(functools.partial(cross_kernel, kv_heads=kv_heads, group=g...  22.5 us
    ppermute x1, waiting for transfers between devices, per_device(): near_on = lax.ppermute(near[:half + cross_rows], 'ctx', [(1, 0), (2, 3)])  11.3 us
    ppermute x1, waiting for transfers between devices, per_device(): pair = lax.ppermute(block, 'ctx', [(0, 1), (1, 0), (2, 3), (3, 2)])  10.6 us
    ppermute x1, waiting for transfers between devices, per_device(): lax.ppermute(piece, 'ctx', [(c, c + 1) for c in range(step - 1, n_ctx - 1)])  5.29 us
    all_to_all x1, starting transfers between devices, per_device(): lax.all_to_all(kv_cross, 'pipe', split_axis=0, concat_axis=0, tiled=True)  5.18 us
    pallas_call x1, Pallas kernels, self_attention(): pl.pallas_call(functools.partial(self_kernel, kv_heads=kv_heads, group=gr...  4.09 us
    ppermute x1, starting transfers between devices, per_device(): lax.ppermute(piece, 'ctx', [(c, c + 1) for c in range(step - 1, n_ctx - 1)])  3.5 us
    ppermute x1, starting transfers between devices, per_device(): pair = lax.ppermute(block, 'ctx', [(0, 1), (1, 0), (2, 3), (3, 2)])  2.48 us
  transfers between devices with their start and end apart: 7, of which 4 were waited for; matrix products, arithmetic and copies ran while one was open for 1% of the time, Pallas kernels for 27%

profile of v1, /device:TPU:0, one launch (start us, length us, event | category | flops | bytes accessed | tf_op | source)
XLA Modules:
  0.0 74.2 jit_solution(3441221065680139389)
XLA Ops:
  0.6 5.2 %all-to-all-start = ((bf16[4,2,64,2,256]{4,3,2,1,0:T(2,128)(2,1)}), bf16[4,2,64,2,256]{4,3,2,1,0:T(2,128)(2,1)S(1)}, u32[]{:S(2)}, u32[]{:S(2)}) async-start(bf16[4,2,64,2,256]{4,3,2,1,0:T(2,128)(2,1)} %param.9), calls=%async_computation | async-start | bytes 1048576 | tf_op jit(solution)/shard_map/all_to_all | solution.py:387
  5.8 1.0 %copy.8 = bf16[32,8,2,256]{3,1,2,0:T(8,128)(2,1)S(1)} copy(bf16[32,8,2,256]{3,2,1,0:T(2,128)(2,1)} %bitcast.23) | data formatting | bytes 524288
  6.8 3.5 %collective-permute-start = (bf16[256,512]{1,0:T(8,128)(2,1)S(1)}, bf16[256,512]{1,0:T(8,128)(2,1)S(1)}, u32[]{:S(2)}, u32[]{:S(2)}) collective-permute-start(bf16[256,512]{1,0:T(8,128)(2,1)S(1)} %bitcast.18), channel_id=1, source_target_pairs={{0,2},{2,4},{4,6},{1,3},{3,5},{5,7},{8,10},{10,12},{12,14},{9,11},... | collective-permute-start | bytes 786440 | tf_op jit(solution)/shard_map/ppermute | solution.py:383
  10.3 5.3 %collective-permute-done.refs_1_ = bf16[256,512]{1,0:T(8,128)(2,1)S(1)} collective-permute-done((bf16[256,512]{1,0:T(8,128)(2,1)S(1)}, bf16[256,512]{1,0:T(8,128)(2,1)S(1)}, u32[]{:S(2)}, u32[]{:S(2)}) %collective-permute-start) | collective-permute-done | bytes 262176 | tf_op jit(solution)/shard_map/ppermute | solution.py:383
  15.6 0.0 copy-start.1
  15.6 0.0 all-to-all-done
  15.6 0.0 copy-start
  15.6 0.0 copy-start.3
  15.6 0.0 copy-start.4
  15.6 0.1 copy.9
  15.7 0.9 %pad_maximum_fusion = bf16[768,512]{1,0:T(8,128)(2,1)} fusion(bf16[128,512]{1,0:T(8,128)(2,1)S(1)} %get-tuple-element.35, bf16[512,512]{1,0:T(8,128)(2,1)S(1)} %bitcast.16, bf16[128,512]{1,0:T(8,128)(2,1)S(1)} %get-tuple-element.34), kind=kLoop, calls=%fused_computation | loop fusion | flops 2359296 | bytes 1572864 | tf_op jit(solution)/shard_map/concatenate | solution.py:402
  16.7 0.0 copy-done.1
  16.7 2.5 %collective-permute-start.2 = (bf16[768,512]{1,0:T(8,128)(2,1)}, bf16[768,512]{1,0:T(8,128)(2,1)S(1)}, u32[]{:S(2)}, u32[]{:S(2)}) collective-permute-start(bf16[768,512]{1,0:T(8,128)(2,1)} %pad_maximum_fusion), channel_id=1, source_target_pairs={{0,2},{2,0},{4,6},{6,4},{1,3},{3,1},{5,7},{7,5},{8,10},{10,8},{12,... | collective-permute-start | bytes 2359304 | tf_op jit(solution)/shard_map/ppermute | solution.py:405
  19.1 0.7 collective-permute-start.1
  19.9 0.1 pad_add_fusion.place_ref
  19.9 0.0 copy-done
  19.9 0.0 copy-done.3
  19.9 0.0 copy-done.4
  19.9 5.2 %shard_map.77 = (f32[8,2,8,256]{3,2,1,0:T(8,128)S(1)}, f32[8,2,128,256]{3,2,1,0:T(8,128)S(1)}) custom-call(s32[1,8]{1,0:T(1,128)S(1)} %copy-done.3, s32[1,8]{1,0:T(1,128)S(1)} %copy-done.4, s32[2]{0:T(128)S(1)} %pad_add_fusion.place_ref, bf16[256,2048]{1,0:T(8,128)(2,1)S(1)} %bitcast.12, bf16[512,512]{1,0:T(8,128)(2,1)S(1)} %bitcast.17), custom_call_target="tpu_custom_call" | custom-call | flops 1073741824 | bytes 2097152 | tf_op jit(solution)/shard_map/pallas_call | solution.py:354
  25.1 10.6 %collective-permute-done.2.refs_0_.refs_3_ = bf16[768,512]{1,0:T(8,128)(2,1)S(1)} collective-permute-done((bf16[768,512]{1,0:T(8,128)(2,1)}, bf16[768,512]{1,0:T(8,128)(2,1)S(1)}, u32[]{:S(2)}, u32[]{:S(2)}) %collective-permute-start.2) | collective-permute-done | bytes 786464 | tf_op jit(solution)/shard_map/ppermute | solution.py:405
  35.8 0.0 collective-permute-done.1.refs_2_.refs_0_
  35.8 1.3 %collective-permute-start.4 = (bf16[640,512]{1,0:T(8,128)(2,1)S(1)}, bf16[640,512]{1,0:T(8,128)(2,1)S(1)}, u32[]{:S(2)}, u32[]{:S(2)}) collective-permute-start(bf16[640,512]{1,0:T(8,128)(2,1)S(1)} %slice.15), channel_id=1, source_target_pairs={{2,0},{4,6},{3,1},{5,7},{10,8},{12,14},{11,9},{13,15},{18,16},{20,... | collective-permute-start | bytes 1966088 | tf_op jit(solution)/shard_map/ppermute | solution.py:409
  37.1 0.7 collective-permute-start.3
  37.8 5.3 %shard_map.78 = (f32[8,2,8,256]{3,2,1,0:T(8,128)S(1)}, f32[8,2,128,256]{3,2,1,0:T(8,128)S(1)}) custom-call(s32[1,8]{1,0:T(1,128)S(1)} %copy-done.3, s32[1,8]{1,0:T(1,128)S(1)} %copy-done.4, s32[2]{0:T(128)S(1)} %pad_add_fusion.place_ref, bf16[256,2048]{1,0:T(8,128)(2,1)S(1)} %bitcast.13, bf16[768,512]{1,0:T(8,128)(2,1)S(1)} %collective-permute-done.2.refs_0_.refs_3_, ...), custom_call_target="tpu_custom_call" | custom-call | flops 1073741824 | bytes 2097152 | tf_op jit(solution)/shard_map/pallas_call | solution.py:354
  43.2 0.0 collective-permute-done.3.refs_0_
  43.2 11.3 %collective-permute-done.4.refs_4_.refs_1_ = bf16[640,512]{1,0:T(8,128)(2,1)S(1)} collective-permute-done((bf16[640,512]{1,0:T(8,128)(2,1)S(1)}, bf16[640,512]{1,0:T(8,128)(2,1)S(1)}, u32[]{:S(2)}, u32[]{:S(2)}) %collective-permute-start.4) | collective-permute-done | bytes 655392 | tf_op jit(solution)/shard_map/ppermute | solution.py:409
  54.5 0.0 copy-start.2
  54.5 0.0 copy-start.5
  54.5 1.4 %collective-permute-start.5 = (bf16[512,512]{1,0:T(8,128)(2,1)S(1)}, bf16[512,512]{1,0:T(8,128)(2,1)S(1)}, u32[]{:S(2)}, u32[]{:S(2)}) collective-permute-start(bf16[512,512]{1,0:T(8,128)(2,1)S(1)} %collective-permute-done.3.refs_0_), channel_id=1, source_target_pairs={{2,0},{4,6},{3,1},{5,7},{10,8},{12,14},{11,9},{13,15},{18,16},{20,... | collective-permute-start | bytes 1572872 | tf_op jit(solution)/shard_map/ppermute | solution.py:412
  55.9 5.4 %shard_map.80 = (f32[8,2,8,256]{3,2,1,0:T(8,128)S(1)}, f32[8,2,128,256]{3,2,1,0:T(8,128)S(1)}) custom-call(s32[1,8]{1,0:T(1,128)S(1)} %copy-done.3, s32[1,8]{1,0:T(1,128)S(1)} %copy-done.4, s32[2]{0:T(128)S(1)} %pad_add_fusion.place_ref, bf16[256,2048]{1,0:T(8,128)(2,1)S(1)} %bitcast.14, bf16[768,512]{1,0:T(8,128)(2,1)S(1)} %collective-permute-done.1.refs_2_.refs_0_, ...), custom_call_target="tpu_custom_call" | custom-call | flops 1073741824 | bytes 2097152 | tf_op jit(solution)/shard_map/pallas_call | solution.py:354
  61.3 0.0 copy-done.2
  61.3 0.0 copy-done.5
  61.3 4.1 %shard_map.79 = bf16[256,2048]{1,0:T(8,128)(2,1)} custom-call(s32[1,8]{1,0:T(1,128)S(1)} %copy-done.3, s32[2]{0:T(128)S(1)} %pad_add_fusion.place_ref, bf16[256,2048]{1,0:T(8,128)(2,1)S(1)} %bitcast.20, bf16[256,512]{1,0:T(8,128)(2,1)S(1)} %bitcast.19, bf16[256,512]{1,0:T(8,128)(2,1)S(1)} %copy-done.2, ...), custom_call_target="tpu_custom_call" | custom-call | flops 3758096384 | bytes 2097152 | tf_op jit(solution)/shard_map/pallas_call | solution.py:323
  65.4 2.1 %collective-permute-done.5.refs_1_ = bf16[512,512]{1,0:T(8,128)(2,1)S(1)} collective-permute-done((bf16[512,512]{1,0:T(8,128)(2,1)S(1)}, bf16[512,512]{1,0:T(8,128)(2,1)S(1)}, u32[]{:S(2)}, u32[]{:S(2)}) %collective-permute-start.5) | collective-permute-done | bytes 524320 | tf_op jit(solution)/shard_map/ppermute | solution.py:412
  67.5 6.7 %shard_map.81 = bf16[256,2048]{1,0:T(8,128)(2,1)} custom-call(s32[1,8]{1,0:T(1,128)S(1)} %copy-done.3, s32[1,8]{1,0:T(1,128)S(1)} %copy-done.4, s32[2]{0:T(128)S(1)} %pad_add_fusion.place_ref, bf16[256,2048]{1,0:T(8,128)(2,1)S(1)} %bitcast.15, bf16[512,512]{1,0:T(8,128)(2,1)S(1)} %collective-permute-done.3.refs_0_, ...), custom_call_target="tpu_custom_call" | custom-call | flops 1073741824 | bytes 2097152 | tf_op jit(solution)/shard_map/pallas_call | solution.py:354
  (3 shorter events, 0.1 us)
Async XLA Ops:
  0.6 15.0 %all-to-all-start = ((bf16[4,2,64,2,256]{4,3,2,1,0:T(2,128)(2,1)}), bf16[4,2,64,2,256]{4,3,2,1,0:T(2,128)(2,1)S(1)}, u32[]{:S(2)}, u32[]{:S(2)}) async-start(bf16[4,2,64,2,256]{4,3,2,1,0:T(2,128)(2,1)} %param.9), calls=%async_computation | async-start | bytes 1048576 | tf_op jit(solution)/shard_map/all_to_all | solution.py:387
  6.8 8.8 %collective-permute-start = (bf16[256,512]{1,0:T(8,128)(2,1)S(1)}, bf16[256,512]{1,0:T(8,128)(2,1)S(1)}, u32[]{:S(2)}, u32[]{:S(2)}) collective-permute-start(bf16[256,512]{1,0:T(8,128)(2,1)S(1)} %bitcast.18), channel_id=1, source_target_pairs={{0,2},{2,4},{4,6},{1,3},{3,5},{5,7},{8,10},{10,12},{12,14},{9,11},... | collective-permute-start | bytes 786440 | tf_op jit(solution)/shard_map/ppermute | solution.py:383
  15.6 1.1 %copy-start.1 = (bf16[256,512]{1,0:T(8,128)(2,1)}, bf16[256,512]{1,0:T(8,128)(2,1)S(1)}, u32[]{:S(2)}) copy-start(bf16[256,512]{1,0:T(8,128)(2,1)S(1)} %collective-permute-done.refs_1_) | copy-start | bytes 786436
  15.6 4.4 %copy-start = (bf16[1,256,2048]{2,1,0:T(8,128)(2,1)S(1)}, bf16[1,256,2048]{2,1,0:T(8,128)(2,1)}, u32[]{:S(2)}) copy-start(bf16[1,256,2048]{2,1,0:T(8,128)(2,1)} %param.8) | copy-start | bytes 3145732
  15.6 4.4 %copy-start.3 = (s32[1,8]{1,0:T(1,128)S(1)}, s32[1,8]{1,0:T(1,128)}, u32[]{:S(2)}) copy-start(s32[1,8]{1,0:T(1,128)} %lengths_ref.9) | copy-start | bytes 100
  15.6 4.4 %copy-start.4 = (s32[1,8]{1,0:T(1,128)S(1)}, s32[1,8]{1,0:T(1,128)}, u32[]{:S(2)}) copy-start(s32[1,8]{1,0:T(1,128)} %images_ref.7) | copy-start | bytes 100
  16.7 19.1 %collective-permute-start.2 = (bf16[768,512]{1,0:T(8,128)(2,1)}, bf16[768,512]{1,0:T(8,128)(2,1)S(1)}, u32[]{:S(2)}, u32[]{:S(2)}) collective-permute-start(bf16[768,512]{1,0:T(8,128)(2,1)} %pad_maximum_fusion), channel_id=1, source_target_pairs={{0,2},{2,0},{4,6},{6,4},{1,3},{3,1},{5,7},{7,5},{8,10},{10,8},{12,... | collective-permute-start | bytes 2359304 | tf_op jit(solution)/shard_map/ppermute | solution.py:405
  19.1 16.6 %collective-permute-start.1 = (bf16[768,512]{1,0:T(8,128)(2,1)}, bf16[768,512]{1,0:T(8,128)(2,1)S(1)}, u32[]{:S(2)}, u32[]{:S(2)}) collective-permute-start(bf16[768,512]{1,0:T(8,128)(2,1)} %pad_maximum_fusion), channel_id=1, source_target_pairs={{2,4},{4,2},{3,5},{5,3},{10,12},{12,10},{11,13},{13,11},{18,20},{2... | collective-permute-start | bytes 2359304 | tf_op jit(solution)/shard_map/ppermute | solution.py:404
  35.8 18.7 %collective-permute-start.4 = (bf16[640,512]{1,0:T(8,128)(2,1)S(1)}, bf16[640,512]{1,0:T(8,128)(2,1)S(1)}, u32[]{:S(2)}, u32[]{:S(2)}) collective-permute-start(bf16[640,512]{1,0:T(8,128)(2,1)S(1)} %slice.15), channel_id=1, source_target_pairs={{2,0},{4,6},{3,1},{5,7},{10,8},{12,14},{11,9},{13,15},{18,16},{20,... | collective-permute-start | bytes 1966088 | tf_op jit(solution)/shard_map/ppermute | solution.py:409
  37.1 6.0 %collective-permute-start.3 = (bf16[512,512]{1,0:T(8,128)(2,1)S(1)}, bf16[512,512]{1,0:T(8,128)(2,1)S(1)}, u32[]{:S(2)}, u32[]{:S(2)}) collective-permute-start(bf16[512,512]{1,0:T(8,128)(2,1)S(1)} %slice.14), channel_id=1, source_target_pairs={{2,4},{4,2},{3,5},{5,3},{10,12},{12,10},{11,13},{13,11},{18,20},{2... | collective-permute-start | bytes 1572872 | tf_op jit(solution)/shard_map/ppermute | solution.py:408
  54.5 6.8 %copy-start.2 = (bf16[256,512]{1,0:T(8,128)(2,1)S(1)}, bf16[256,512]{1,0:T(8,128)(2,1)}, u32[]{:S(2)}) copy-start(bf16[256,512]{1,0:T(8,128)(2,1)} %copy-done.1) | copy-start | bytes 786436
  54.5 6.8 %copy-start.5 = (bf16[1,256,2048]{2,1,0:T(8,128)(2,1)S(1)}, bf16[1,256,2048]{2,1,0:T(8,128)(2,1)}, u32[]{:S(2)}) copy-start(bf16[1,256,2048]{2,1,0:T(8,128)(2,1)} %param.6) | copy-start | bytes 3145732
  54.5 13.0 %collective-permute-start.5 = (bf16[512,512]{1,0:T(8,128)(2,1)S(1)}, bf16[512,512]{1,0:T(8,128)(2,1)S(1)}, u32[]{:S(2)}, u32[]{:S(2)}) collective-permute-start(bf16[512,512]{1,0:T(8,128)(2,1)S(1)} %collective-permute-done.3.refs_0_), channel_id=1, source_target_pairs={{2,0},{4,6},{3,1},{5,7},{10,8},{12,14},{11,9},{13,15},{18,16},{20,... | collective-permute-start | bytes 1572872 | tf_op jit(solution)/shard_map/ppermute | solution.py:412

commit v2 on v1

--- a/solution.py
+++ b/solution.py
@@ -79,10 +79,15 @@
     flipped_at[...] = ref[rows, (kv_heads + g) * HD : (kv_heads + g + 1) * HD].T
 
 
-def self_kernel(lengths_ref, place_ref, q_ref, *refs, kv_heads, group, spans, parts, samples):
-    sources = {part[1] for part in parts}
-    pieces = refs[: len(sources)]
-    out_ref, stat_ref, mixed_ref, keys_ref, flipped_ref = refs[len(sources) :]
+def self_kernel(
+    lengths_ref, place_ref, q_ref, *refs, kv_heads, group, spans, parts, samples, begin, end
+):
+    refs = list(refs)
+    take = lambda n: [refs.pop(0) for _ in range(n)]
+    pieces = take(len({part[1] for part in parts}))
+    stat_in, mixed_in = (None, None) if begin else take(2)
+    out_ref = take(1)[0] if end else None
+    stat_ref, mixed_ref, keys_ref, flipped_ref = take(4)
     rows_here = q_ref.shape[0]
     tiles = rows_here // TILE
     height = group * TILE
@@ -99,17 +104,17 @@
 
     def limits(number):
         back, count = spans[number]
-        end = base - (back - 1) * rows_here
-        return end - count, end
+        past = base - (back - 1) * rows_here
+        return past - count, past
 
     def reached(number):
-        start, end = limits(number)
+        start, past = limits(number)
         many = jnp.int32(0)
         for low in lows:
-            many = many + (low < end).astype(jnp.int32)
+            many = many + (low < past).astype(jnp.int32)
         return jnp.where(start >= 0, many, 0)
 
-    counts = [reached(number) for number in range(1, len(spans))]
+    counts = [reached(number) for number in range(len(spans))]
     for number, source, at, offset, count, only in parts:
 
         def fill(number=number, source=source, at=at, offset=offset, count=count):
@@ -120,10 +125,10 @@
                     slice(at, at + count), kv_heads, g,
                 )
 
-        if number == 0:
+        if spans[number][0] == 0:
             fill()
         else:
-            asked = counts[number - 1] > 0
+            asked = counts[number] > 0
             if only is not None:
                 asked = asked & (place_ref[0] == only)
             pl.when(asked)(fill)
@@ -153,16 +158,20 @@
         s = jnp.where((key_t >= row_start) & (key_t <= row_t), s, LOW)
         keep(tile, g, absorb(None, s, flipped_ref[g, :, : own_count(tile)]))
 
-    staggered(
-        [(tile, g) for tile in range(tiles) for g in range(kv_heads)], own_scores, own_finish
-    )
+    if begin:
+        staggered(
+            [(tile, g) for tile in range(tiles) for g in range(kv_heads)], own_scores, own_finish
+        )
+    else:
+        stat_ref[...] = stat_in[...]
+        mixed_ref[...] = mixed_in[...]
 
     together = math.gcd(tiles, TOGETHER)
-    for number in range(1, len(spans)):
+    for number in range(1 if begin else 0, len(spans)):
         start, _ = limits(number)
         at, count = ats[number], spans[number][1]
 
-        @pl.loop(0, (counts[number - 1] + together - 1) // together)
+        @pl.loop(0, (counts[number] + together - 1) // together)
         def _(turn, start=start, at=at, count=count):
             def scores(n, g):
                 q = stacked_queries(q_ref, turn * together + n, g, group)
@@ -180,7 +189,7 @@
                 [(n, g) for n in range(together) for g in range(kv_heads)], scores, finish
             )
 
-    for tile in range(tiles):
+    for tile in range(tiles if end else 0):
         for g in range(kv_heads):
             write_heads(out_ref, mixed_ref[tile, g], stat_ref[tile, g, 1:2, :], tile, g, group)
 
@@ -317,57 +326,97 @@
     return (tiles, kv_heads, 8, height), (tiles, kv_heads, HD, height)
 
 
-def self_attention(lengths, place, q, pieces, spans, parts, kv_heads, group):
+def state_call(kernel, operands, rows, width, keys, shapes, scratch, end, dtype):
+    scalars = sum(x.dtype == jnp.int32 for x in operands)
+    state_scratch = []
+    if end:
+        out_shape = jax.ShapeDtypeStruct((rows, width), dtype)
+        state_scratch = [pltpu.VMEM(s, jnp.float32) for s in shapes]
+    else:
+        out_shape = [jax.ShapeDtypeStruct(s, jnp.float32) for s in shapes]
+    return pl.pallas_call(
+        kernel,
+        out_shape=out_shape,
+        in_specs=[smem()] * scalars + [vmem()] * (len(operands) - scalars),
+        out_specs=vmem() if end else [vmem(), vmem()],
+        scratch_shapes=state_scratch + scratch,
+        compiler_params=pltpu.CompilerParams(vmem_limit_bytes=28 << 20),
+        cost_estimate=cost(rows, width, keys),
+    )(*operands)
+
+
+def self_attention(lengths, place, q, pieces, spans, parts, state, end, kv_heads, group):
     rows, width = q.shape
     keys = sum(count for _, count in spans)
-    return pl.pallas_call(
-        functools.partial(
-            self_kernel, kv_heads=kv_heads, group=group, spans=spans, parts=parts,
-            samples=lengths.shape[1],
-        ),
-        out_shape=jax.ShapeDtypeStruct((rows, width), q.dtype),
-        in_specs=[smem(), smem(), vmem()] + [vmem() for p in pieces],
-        out_specs=vmem(),
-        scratch_shapes=[pltpu.VMEM(s, jnp.float32) for s in state_shapes(rows, kv_heads, group)]
-        + [
-            pltpu.VMEM((kv_heads, keys, HD), q.dtype),
-            pltpu.VMEM((kv_heads, HD, keys), q.dtype),
-        ],
-        compiler_params=pltpu.CompilerParams(vmem_limit_bytes=28 << 20),
-        cost_estimate=cost(rows, width, keys),
-    )(lengths, place, q, *pieces)
+    begin = state is None
+    kernel = functools.partial(
+        self_kernel, kv_heads=kv_heads, group=group, spans=spans, parts=parts,
+        samples=lengths.shape[1], begin=begin, end=end,
+    )
+    scratch = [
+        pltpu.VMEM((kv_heads, keys, HD), q.dtype), pltpu.VMEM((kv_heads, HD, keys), q.dtype)
+    ]
+    operands = (lengths, place, q, *pieces, *(() if begin else state))
+    shapes = state_shapes(rows, kv_heads, group)
+    return state_call(kernel, operands, rows, width, keys, shapes, scratch, end, q.dtype)
 
 
 def cross_attention(lengths, images, place, q, sources, state, end, kv_heads, group, image_count):
     rows, width = q.shape
     begin = state is None
-    state = () if begin else state
+    kernel = functools.partial(
+        cross_kernel, kv_heads=kv_heads, group=group,
+        sources=tuple(tuple(piece[1:] for piece in source) for source in sources),
+        samples=lengths.shape[1], begin=begin, end=end,
+    )
+    pieces = [piece[0] for source in sources for piece in source]
+    keys = sum(source[0][2] * source[0][3] for source in sources)
+    scratch = [
+        pltpu.VMEM((image_count, kv_heads, keys, HD), q.dtype),
+        pltpu.VMEM((image_count, kv_heads, HD, keys), q.dtype),
+    ]
+    operands = (lengths, images, place, q, *pieces, *(() if begin else state))
     shapes = state_shapes(rows, kv_heads, group)
-    state_scratch = []
-    if end:
-        out_shape = jax.ShapeDtypeStruct((rows, width), q.dtype)
-        state_scratch = [pltpu.VMEM(s, jnp.float32) for s in shapes]
-    else:
-        out_shape = [jax.ShapeDtypeStruct(s, jnp.float32) for s in shapes]
-    operands = [piece[0] for source in sources for piece in source]
-    keys = sum(source[0][2] * source[0][3] for source in sources)
+    return state_call(kernel, operands, rows, width, keys, shapes, scratch, end, q.dtype)
+
+
+def cross_ending(lengths, images, place, q, sources, state, rest, head, kv_heads, group, image_count):
+    rows, width = q.shape
+    share = width // kv_heads
+    keys = sources[0][2] * sources[0][3]
+    kernel = functools.partial(
+        cross_kernel, kv_heads=1, group=group,
+        sources=(tuple(piece[1:] for piece in sources),),
+        samples=lengths.shape[1], begin=False, end=True,
+    )
+    pieces = [piece[0] for piece in sources]
+    shapes = state_shapes(rows, 1, group)
+    first = lambda shape: pl.BlockSpec(shape, lambda i: (0, head) + (0,) * (len(shape) - 2))
+    body = lambda *refs: kernel(*refs)
+    operands = [lengths, images, place, q, *pieces, *state]
+    in_specs = [smem()] * 3 + [first((rows, share))] + [vmem()] * len(pieces)
+    in_specs += [first(shape) for shape in shapes]
+    aliases = {}
+    if rest is not None:
+        body = lambda *refs: kernel(*refs[: len(operands) - 1], *refs[len(operands) :])
+        aliases = {len(operands): 0}
+        operands.append(rest)
+        in_specs.append(pl.BlockSpec(memory_space=pl.ANY))
     return pl.pallas_call(
-        functools.partial(
-            cross_kernel, kv_heads=kv_heads, group=group,
-            sources=tuple(tuple(piece[1:] for piece in source) for source in sources),
-            samples=lengths.shape[1], begin=begin, end=end,
-        ),
-        out_shape=out_shape,
-        in_specs=[smem(), smem(), smem(), vmem()] + [vmem() for p in (*operands, *state)],
-        out_specs=vmem() if end else [vmem(), vmem()],
-        scratch_shapes=state_scratch
+        body,
+        out_shape=jax.ShapeDtypeStruct((rows, width), q.dtype),
+        grid=(1,),
+        in_specs=in_specs,
+        out_specs=first((rows, share)),
+        scratch_shapes=[pltpu.VMEM(s, jnp.float32) for s in shapes]
         + [
-            pltpu.VMEM((image_count, kv_heads, keys, HD), q.dtype),
-            pltpu.VMEM((image_count, kv_heads, HD, keys), q.dtype),
+            pltpu.VMEM((image_count, 1, keys, HD), q.dtype),
+            pltpu.VMEM((image_count, 1, HD, keys), q.dtype),
         ],
+        input_output_aliases=aliases,
         compiler_params=pltpu.CompilerParams(vmem_limit_bytes=28 << 20),
-        cost_estimate=cost(rows, width, keys),
-    )(lengths, images, place, q, *operands, *state)
+        cost_estimate=cost(rows, share, keys),
+    )(*operands)
 
 
 def per_device(q_self, kv_self, q_cross, kv_cross, sample_lengths, sample_image, *, n_pipe, n_ctx):
@@ -379,13 +428,14 @@
     inner = ((z == 1) | (z == 2)).astype(jnp.int32)
     place = jnp.stack([z, inner]).astype(jnp.int32)
 
-    own = kv_self[0].reshape(rows, -1)
     shift = lambda piece, step: lax.ppermute(
         piece, "ctx", [(c, c + 1) for c in range(step - 1, n_ctx - 1)]
     )
-    passed = shift(own, 1)
+    passed = shift(kv_self[0], 1)
     arrived = lax.all_to_all(kv_cross, "pipe", split_axis=0, concat_axis=0, tiled=True)
     arrived, passed = lax.optimization_barrier((arrived, passed))
+    own = kv_self[0].reshape(rows, -1)
+    passed = passed.reshape(rows, -1)
     own_rows = arrived.reshape(-1, own.shape[1])
     cross_rows = own_rows.shape[0]
     longest = rows * n_ctx * 5 // 8
@@ -403,27 +453,42 @@
         at = lambda array, row: (array, row, n_pipe, each)
         near = lax.ppermute(block, "ctx", [(1, 2), (2, 1)])
         pair = lax.ppermute(block, "ctx", [(0, 1), (1, 0), (2, 3), (3, 2)])
+        early = ((0, rows), (1, rows))
+        parts = ((0, 0, 0, 0, rows, None), (1, 1, 0, 0, rows, None))
         state = attend_cross([[at(own_rows, 0)]], None, False)
-        near, pair, state = lax.optimization_barrier((near, pair, state))
-        far = lax.ppermute(pair[half : half + cross_rows], "ctx", [(1, 2), (2, 1)])
+        self_state = attend_self([own, passed], early, parts, None, False)
+        near, pair, state, self_state = lax.optimization_barrier((near, pair, state, self_state))
+        columns = lambda j: pair[half : half + cross_rows, j * HD : (j + 1) * HD]
+        far = [
+            lax.ppermute(
+                jnp.concatenate([columns(g), columns(kv_heads + g)], axis=1),
+                "ctx", [(1, 2), (2, 1)],
+            )
+            for g in range(kv_heads)
+        ]
         near_on = lax.ppermute(near[: half + cross_rows], "ctx", [(1, 0), (2, 3)])
         state = attend_cross([[at(pair, half)]], state, False)
-        far, near_on, state = lax.optimization_barrier((far, near_on, state))
-        far_on = lax.ppermute(far, "ctx", [(1, 0), (2, 3)])
+        far[0], state = lax.optimization_barrier((far[0], state))
+        low = half + cross_rows
+        parts = (
+            (0, 0, low, 0, half, 2),
+            (0, 0, 0, half, half, 2),
+            (0, 1, low, 0, half, 3),
+            (0, 1, 0, half, half, 3),
+        )
+        self_state = attend_self([near, pair], ((2, rows),), parts, self_state, False)
+        far[-1], self_state = lax.optimization_barrier((far[-1], self_state))
+        far_on = [lax.ppermute(part, "ctx", [(1, 0), (2, 3)]) for part in far]
         state = attend_cross([[at(near, half), at(near_on, half)]], state, False)
-        low = half + cross_rows
-        spans = ((0, rows), (1, rows), (2, rows), (3, half))
-        parts = (
-            (0, 0, 0, 0, rows, None),
-            (1, 1, 0, 0, rows, None),
-            (2, 2, low, 0, half, 2),
-            (2, 2, 0, half, half, 2),
-            (2, 3, low, 0, half, 3),
-            (2, 3, 0, half, half, 3),
-            (3, 4, 0, 0, half, 3),
-        )
-        self_out = attend_self([own, passed, near, pair, near_on], spans, parts)
-        cross_out = attend_cross([[at(far, 0), at(far_on, 0)]], state, True)
+        parts = ((0, 0, 0, 0, half, 3),)
+        self_out = attend_self([near_on], ((3, half),), parts, self_state, True)
+        cross_out = None
+        for g in range(kv_heads):
+            cross_out = cross_ending(
+                sample_lengths, sample_image, place, q_cross[0],
+                [at(far[g], 0), at(far_on[g], 0)], state, cross_out, g,
+                kv_heads, group, image_count,
+            )
     else:
         pieces, spans, left, step = [own, passed], [(0, rows), (1, rows)], longest - 1 - rows, 1
         while left > 0 and step < n_ctx - 1:
@@ -433,7 +498,7 @@
             spans.append((step, count))
             left -= rows
         parts = tuple((n, n, 0, 0, count, None) for n, (_, count) in enumerate(spans))
-        self_out = attend_self(pieces, tuple(spans), parts)
+        self_out = attend_self(pieces, tuple(spans), parts, None, True)
         gathered = lax.all_gather(own_rows, "ctx", axis=0, tiled=True)
         cross_out = attend_cross([[(gathered, 0, n_ctx * n_pipe, each)]], None, True)
     return self_out[None], cross_out[None]

time: 74.6 us -> 75.6 us (1.013); the launches traced: 74.2 us -> 76.6 us
  waiting for transfers between devices: 29.3 us -> 21.7 us
  Pallas kernels: 26.6 us -> 33.3 us
  local copies, waits for them, and re-layouts: 1.19 us -> 3.63 us
  starting transfers between devices: 15.3 us -> 17 us
  other arithmetic: 1.01 us -> 0.14 us
    pallas_call x5 -> x8, Pallas kernels: 26.6 us -> 33.3 us  [the longest x6 22.8 us: state_call(): pl.pallas_call(kernel, out_shape=out_shape, in_specs=[smem()] * scalars +...]
    ppermute x1, waiting for transfers between devices: 10.6 us -> 6.58 us  [per_device(): pair = lax.ppermute(block, 'ctx', [(0, 1), (1, 0), (2, 3), (3, 2)])]
    ppermute x2 -> x4, waiting for transfers between devices: 2.06 us -> 0.01 us  [the longest x2 0.01 us: per_device(): lax.ppermute(jnp.concatenate([columns(g), columns(kv_heads + g)], axis=1)...]
    ppermute x1, waiting for transfers between devices: 11.3 us -> 9.45 us  [per_device(): near_on = lax.ppermute(near[:half + cross_rows], 'ctx', [(1, 0), (2, 3)])]
    ppermute x2 -> x4, starting transfers between devices: 2.11 us -> 3.94 us  [the longest x2 2.58 us: per_device(): far_on = [lax.ppermute(part, 'ctx', [(1, 0), (2, 3)]) for part in far]]
    unnamed x14 -> x15, local copies, waits for them, and re-layouts: 1.09 us -> 2.65 us
    concatenate x1 -> x2, other arithmetic: 0.93 us -> 0.06 us  [per_device(): jnp.concatenate([columns(g), columns(kv_heads + g)], axis=1)]
  transfers between devices with their start and end apart: 7 -> 9, of which waited for: 4 -> 3; matrix products, arithmetic and copies ran while one was open for 1% -> 2% of each run, Pallas kernels for 27% -> 37%
where the time goes in v2:
time: 75.6 us; the launch traced here: 76.6 us
  Pallas kernels  33.3 us (44%)
  waiting for transfers between devices  21.7 us (29%)
  starting transfers between devices  17 us (22%)
  local copies, waits for them, and re-layouts  3.63 us (5%)
  between operations  0.89 us (1%)
    pallas_call x6, Pallas kernels, state_call(): pl.pallas_call(kernel, out_shape=out_shape, in_specs=[smem()] * scalars +...  22.8 us
    pallas_call x2, Pallas kernels, cross_ending(): pl.pallas_call(body, out_shape=jax.ShapeDtypeStruct((rows, width), q.dtyp...  10.5 us
    ppermute x1, waiting for transfers between devices, per_device(): near_on = lax.ppermute(near[:half + cross_rows], 'ctx', [(1, 0), (2, 3)])  9.45 us
    ppermute x1, waiting for transfers between devices, per_device(): pair = lax.ppermute(block, 'ctx', [(0, 1), (1, 0), (2, 3), (3, 2)])  6.58 us
    ppermute x1, waiting for transfers between devices, per_device(): lax.ppermute(piece, 'ctx', [(c, c + 1) for c in range(step - 1, n_ctx - 1)])  5.62 us
    all_to_all x1, starting transfers between devices, per_device(): lax.all_to_all(kv_cross, 'pipe', split_axis=0, concat_axis=0, tiled=True)  5.18 us
    ppermute x1, starting transfers between devices, per_device(): lax.ppermute(piece, 'ctx', [(c, c + 1) for c in range(step - 1, n_ctx - 1)])  3.49 us
    unnamed x15, local copies, waits for them, and re-layouts  2.65 us
  transfers between devices with their start and end apart: 9, of which 3 were waited for; matrix products, arithmetic and copies ran while one was open for 2% of the time, Pallas kernels for 37%

profile of v2, /device:TPU:0, one launch (start us, length us, event | category | flops | bytes accessed | tf_op | source)
XLA Modules:
  0.0 76.6 jit_solution(1866860201657652060)
XLA Ops:
  0.6 5.2 %all-to-all-start = ((bf16[4,2,64,2,256]{4,3,2,1,0:T(2,128)(2,1)}), bf16[4,2,64,2,256]{4,3,2,1,0:T(2,128)(2,1)S(1)}, u32[]{:S(2)}, u32[]{:S(2)}) async-start(bf16[4,2,64,2,256]{4,3,2,1,0:T(2,128)(2,1)} %param.9), calls=%async_computation | async-start | bytes 1048576 | tf_op jit(solution)/shard_map/all_to_all | solution.py:435
  5.8 3.5 %collective-permute-start = (bf16[256,2,256]{2,1,0:T(2,128)(2,1)}, bf16[256,2,256]{2,1,0:T(2,128)(2,1)S(1)}, u32[]{:S(2)}, u32[]{:S(2)}) collective-permute-start(bf16[256,2,256]{2,1,0:T(2,128)(2,1)} %bitcast.39), channel_id=1, source_target_pairs={{0,2},{2,4},{4,6},{1,3},{3,5},{5,7},{8,10},{10,12},{12,14},{9,11},... | collective-permute-start | bytes 786440 | tf_op jit(solution)/shard_map/ppermute | solution.py:431
  9.3 5.6 %collective-permute-done = bf16[256,2,256]{2,1,0:T(2,128)(2,1)S(1)} collective-permute-done((bf16[256,2,256]{2,1,0:T(2,128)(2,1)}, bf16[256,2,256]{2,1,0:T(2,128)(2,1)S(1)}, u32[]{:S(2)}, u32[]{:S(2)}) %collective-permute-start) | collective-permute-done | bytes 262176 | tf_op jit(solution)/shard_map/ppermute | solution.py:431
  14.9 0.0 all-to-all-done
  14.9 0.1 copy.10
  15.0 0.0 copy-start
  15.0 0.0 copy-start.2
  15.0 0.0 copy-start.3
  15.0 0.2 fusion.1
  15.3 0.7 constant_dynamic-update-slice_fusion.2
  16.0 0.8 %constant_dynamic-update-slice_fusion.1 = bf16[768,512]{1,0:T(8,128)(2,1)} fusion(bf16[768,512]{1,0:T(8,128)(2,1)} %constant_dynamic-update-slice_fusion.2, bf16[512,512]{1,0:T(8,128)(2,1)S(1)} %bitcast.27), kind=kLoop, calls=%fused_computation.3 | loop fusion | bytes 1048576
  16.8 0.7 constant_dynamic-update-slice_fusion
  17.4 2.4 %collective-permute-start.2 = (bf16[768,512]{1,0:T(8,128)(2,1)}, bf16[768,512]{1,0:T(8,128)(2,1)S(1)}, u32[]{:S(2)}, u32[]{:S(2)}) collective-permute-start(bf16[768,512]{1,0:T(8,128)(2,1)} %constant_dynamic-update-slice_fusion), channel_id=1, source_target_pairs={{0,2},{2,0},{4,6},{6,4},{1,3},{3,1},{5,7},{7,5},{8,10},{10,8},{12,... | collective-permute-start | bytes 2359304 | tf_op jit(solution)/shard_map/ppermute | solution.py:455
  19.8 0.7 collective-permute-start.1
  20.5 1.0 %copy.12 = bf16[32,8,2,256]{3,1,2,0:T(8,128)(2,1)S(1)} copy(bf16[32,8,2,256]{3,2,1,0:T(2,128)(2,1)} %bitcast.40) | data formatting | bytes 524288
  21.5 0.1 pad_add_fusion.place_ref.refs_2_
  21.6 0.0 copy-start.1
  21.7 0.0 copy-done
  21.7 0.0 copy-done.2
  21.7 0.0 copy-done.3
  21.7 5.6 %shard_map.77 = (f32[8,2,8,256]{3,2,1,0:T(8,128)S(1)}, f32[8,2,128,256]{3,2,1,0:T(8,128)S(1)}) custom-call(s32[1,8]{1,0:T(1,128)S(1)} %copy-done.2, s32[1,8]{1,0:T(1,128)S(1)} %copy-done.3, s32[2]{0:T(128)S(1)} %pad_add_fusion.place_ref.refs_2_, bf16[256,2048]{1,0:T(8,128)(2,1)S(1)} %bitcast.19, bf16[512,512]{1,0:T(8,128)(2,1)S(1)} %bitcast.28), custom_call_target="tpu_custom_call" | custom-call | flops 1073741824 | bytes 2097152 | tf_op jit(solution)/shard_map/pallas_call | solution.py:337
  27.3 0.0 copy-done.1
  27.3 2.5 %shard_map.78 = (f32[8,2,8,256]{3,2,1,0:T(8,128)S(1)}, f32[8,2,128,256]{3,2,1,0:T(8,128)S(1)}) custom-call(s32[1,8]{1,0:T(1,128)S(1)} %copy-done.2, s32[2]{0:T(128)S(1)} %pad_add_fusion.place_ref.refs_2_, bf16[256,2048]{1,0:T(8,128)(2,1)S(1)} %bitcast.24, bf16[256,512]{1,0:T(8,128)(2,1)S(1)} %bitcast.29, bf16[256,512]{1,0:T(8,128)(2,1)S(1)} %bitcast.30), custom_call_target="tpu_custom_call" | custom-call | flops 2147483648 | bytes 2097152 | tf_op jit(solution)/shard_map/pallas_call | solution.py:337
  29.9 6.6 %collective-permute-done.2.refs_1_.refs_0_ = bf16[768,512]{1,0:T(8,128)(2,1)S(1)} collective-permute-done((bf16[768,512]{1,0:T(8,128)(2,1)}, bf16[768,512]{1,0:T(8,128)(2,1)S(1)}, u32[]{:S(2)}, u32[]{:S(2)}) %collective-permute-start.2) | collective-permute-done | bytes 786464 | tf_op jit(solution)/shard_map/ppermute | solution.py:455
  36.4 0.0 collective-permute-done.1.refs_0_
  36.5 1.3 %collective-permute-start.3 = (bf16[640,512]{1,0:T(8,128)(2,1)S(1)}, bf16[640,512]{1,0:T(8,128)(2,1)S(1)}, u32[]{:S(2)}, u32[]{:S(2)}) collective-permute-start(bf16[640,512]{1,0:T(8,128)(2,1)S(1)} %slice.31), channel_id=1, source_target_pairs={{2,0},{4,6},{3,1},{5,7},{10,8},{12,14},{11,9},{13,15},{18,16},{20,... | collective-permute-start | bytes 1966088 | tf_op jit(solution)/shard_map/ppermute | solution.py:469
  37.8 0.1 fusion
  37.9 0.7 collective-permute-start.6
  38.7 0.7 collective-permute-start.4
  39.3 5.8 %shard_map.81 = (f32[8,2,8,256]{3,2,1,0:T(8,128)S(1)}, f32[8,2,128,256]{3,2,1,0:T(8,128)S(1)}) custom-call(s32[1,8]{1,0:T(1,128)S(1)} %copy-done.2, s32[1,8]{1,0:T(1,128)S(1)} %copy-done.3, s32[2]{0:T(128)S(1)} %pad_add_fusion.place_ref.refs_2_, bf16[256,2048]{1,0:T(8,128)(2,1)S(1)} %bitcast.20, bf16[768,512]{1,0:T(8,128)(2,1)S(1)} %collective-permute-done.2.refs_1_.refs_0_, ...), custom_call_target="tpu_custom_call" | custom-call | flops 1073741824 | bytes 2097152 | tf_op jit(solution)/shard_map/pallas_call | solution.py:337
  45.1 0.0 collective-permute-done.6.refs_4_
  45.1 1.3 %collective-permute-start.7 = (bf16[512,256]{1,0:T(8,128)(2,1)S(1)}, bf16[512,256]{1,0:T(8,128)(2,1)S(1)}, u32[]{:S(2)}, u32[]{:S(2)}) collective-permute-start(bf16[512,256]{1,0:T(8,128)(2,1)S(1)} %collective-permute-done.6.refs_4_), channel_id=1, source_target_pairs={{2,0},{4,6},{3,1},{5,7},{10,8},{12,14},{11,9},{13,15},{18,16},{20,... | collective-permute-start | bytes 786440 | tf_op jit(solution)/shard_map/ppermute | solution.py:481
  46.4 1.0 %shard_map.79 = (f32[8,2,8,256]{3,2,1,0:T(8,128)S(1)}, f32[8,2,128,256]{3,2,1,0:T(8,128)S(1)}) custom-call(s32[1,8]{1,0:T(1,128)S(1)} %copy-done.2, s32[2]{0:T(128)S(1)} %pad_add_fusion.place_ref.refs_2_, bf16[256,2048]{1,0:T(8,128)(2,1)S(1)} %bitcast.25, bf16[768,512]{1,0:T(8,128)(2,1)S(1)} %collective-permute-done.1.refs_0_, ...), custom_call_target="tpu_custom_call" | custom-call | flops 1073741824 | bytes 2097152 | tf_op jit(solution)/shard_map/pallas_call | solution.py:337
  47.4 0.0 collective-permute-done.4.refs_4_
  47.4 1.3 %collective-permute-start.5 = (bf16[512,256]{1,0:T(8,128)(2,1)S(1)}, bf16[512,256]{1,0:T(8,128)(2,1)S(1)}, u32[]{:S(2)}, u32[]{:S(2)}) collective-permute-start(bf16[512,256]{1,0:T(8,128)(2,1)S(1)} %collective-permute-done.4.refs_4_), channel_id=1, source_target_pairs={{2,0},{4,6},{3,1},{5,7},{10,8},{12,14},{11,9},{13,15},{18,16},{20,... | collective-permute-start | bytes 786440 | tf_op jit(solution)/shard_map/ppermute | solution.py:481
  48.7 9.5 %collective-permute-done.3.refs_0_.refs_1_ = bf16[640,512]{1,0:T(8,128)(2,1)S(1)} collective-permute-done((bf16[640,512]{1,0:T(8,128)(2,1)S(1)}, bf16[640,512]{1,0:T(8,128)(2,1)S(1)}, u32[]{:S(2)}, u32[]{:S(2)}) %collective-permute-start.3) | collective-permute-done | bytes 655392 | tf_op jit(solution)/shard_map/ppermute | solution.py:469
  58.2 2.1 %shard_map.80 = bf16[256,2048]{1,0:T(8,128)(2,1)} custom-call(s32[1,8]{1,0:T(1,128)S(1)} %copy-done.2, s32[2]{0:T(128)S(1)} %pad_add_fusion.place_ref.refs_2_, bf16[256,2048]{1,0:T(8,128)(2,1)S(1)} %bitcast.26, bf16[640,512]{1,0:T(8,128)(2,1)S(1)} %collective-permute-done.3.refs_0_.refs_1_, f32[8,2,8,256]{3,2,1,0:T(8,128)S(1)} %get-tuple-element.38.refs_1_, ...), custom_call_target="tpu_custom_call" | custom-call | flops 536870912 | bytes 2097152 | tf_op jit(solution)/shard_map/pallas_call | solution.py:337
  60.3 5.8 %shard_map.82 = (f32[8,2,8,256]{3,2,1,0:T(8,128)S(1)}, f32[8,2,128,256]{3,2,1,0:T(8,128)S(1)}) custom-call(s32[1,8]{1,0:T(1,128)S(1)} %copy-done.2, s32[1,8]{1,0:T(1,128)S(1)} %copy-done.3, s32[2]{0:T(128)S(1)} %pad_add_fusion.place_ref.refs_2_, bf16[256,2048]{1,0:T(8,128)(2,1)S(1)} %bitcast.21, bf16[768,512]{1,0:T(8,128)(2,1)S(1)} %collective-permute-done.1.refs_0_, ...), custom_call_target="tpu_custom_call" | custom-call | flops 1073741824 | bytes 2097152 | tf_op jit(solution)/shard_map/pallas_call | solution.py:337
  66.1 0.0 collective-permute-done.7.refs_5_
  66.1 5.2 %shard_map.83.refs_8_ = bf16[256,2048]{1,0:T(8,128)(2,1)} custom-call(s32[1,8]{1,0:T(1,128)S(1)} %copy-done.2, s32[1,8]{1,0:T(1,128)S(1)} %copy-done.3, s32[2]{0:T(128)S(1)} %pad_add_fusion.place_ref.refs_2_, bf16[256,2048]{1,0:T(8,128)(2,1)S(1)} %bitcast.22, bf16[512,256]{1,0:T(8,128)(2,1)S(1)} %collective-permute-done.6.refs_4_, ...), custom_call_target="tpu_custom_call" | custom-call | flops 536870912 | bytes 1048576 | tf_op jit(solution)/shard_map/pallas_call | solution.py:405
  71.4 0.0 collective-permute-done.5.refs_5_
  71.4 5.2 %shard_map.84 = bf16[256,2048]{1,0:T(8,128)(2,1)} custom-call(s32[1,8]{1,0:T(1,128)S(1)} %copy-done.2, s32[1,8]{1,0:T(1,128)S(1)} %copy-done.3, s32[2]{0:T(128)S(1)} %pad_add_fusion.place_ref.refs_2_, bf16[256,2048]{1,0:T(8,128)(2,1)S(1)} %bitcast.23, bf16[512,256]{1,0:T(8,128)(2,1)S(1)} %collective-permute-done.4.refs_4_, ...), custom_call_target="tpu_custom_call", output_to_operand_aliasing={{}: (8, {})} | custom-call | flops 536870912 | bytes 1048576 | tf_op jit(solution)/shard_map/pallas_call | solution.py:405
  (6 shorter events, 0.2 us)
Async XLA Ops:
  0.6 14.3 %all-to-all-start = ((bf16[4,2,64,2,256]{4,3,2,1,0:T(2,128)(2,1)}), bf16[4,2,64,2,256]{4,3,2,1,0:T(2,128)(2,1)S(1)}, u32[]{:S(2)}, u32[]{:S(2)}) async-start(bf16[4,2,64,2,256]{4,3,2,1,0:T(2,128)(2,1)} %param.9), calls=%async_computation | async-start | bytes 1048576 | tf_op jit(solution)/shard_map/all_to_all | solution.py:435
  5.8 9.1 %collective-permute-start = (bf16[256,2,256]{2,1,0:T(2,128)(2,1)}, bf16[256,2,256]{2,1,0:T(2,128)(2,1)S(1)}, u32[]{:S(2)}, u32[]{:S(2)}) collective-permute-start(bf16[256,2,256]{2,1,0:T(2,128)(2,1)} %bitcast.39), channel_id=1, source_target_pairs={{0,2},{2,4},{4,6},{1,3},{3,5},{5,7},{8,10},{10,12},{12,14},{9,11},... | collective-permute-start | bytes 786440 | tf_op jit(solution)/shard_map/ppermute | solution.py:431
  15.0 6.6 %copy-start = (bf16[1,256,2048]{2,1,0:T(8,128)(2,1)S(1)}, bf16[1,256,2048]{2,1,0:T(8,128)(2,1)}, u32[]{:S(2)}) copy-start(bf16[1,256,2048]{2,1,0:T(8,128)(2,1)} %param.8) | copy-start | bytes 3145732
  15.0 6.6 %copy-start.2 = (s32[1,8]{1,0:T(1,128)S(1)}, s32[1,8]{1,0:T(1,128)}, u32[]{:S(2)}) copy-start(s32[1,8]{1,0:T(1,128)} %refs_0_.3) | copy-start | bytes 100
  15.0 6.6 %copy-start.3 = (s32[1,8]{1,0:T(1,128)S(1)}, s32[1,8]{1,0:T(1,128)}, u32[]{:S(2)}) copy-start(s32[1,8]{1,0:T(1,128)} %refs_1_.3) | copy-start | bytes 100
  17.4 19.0 %collective-permute-start.2 = (bf16[768,512]{1,0:T(8,128)(2,1)}, bf16[768,512]{1,0:T(8,128)(2,1)S(1)}, u32[]{:S(2)}, u32[]{:S(2)}) collective-permute-start(bf16[768,512]{1,0:T(8,128)(2,1)} %constant_dynamic-update-slice_fusion), channel_id=1, source_target_pairs={{0,2},{2,0},{4,6},{6,4},{1,3},{3,1},{5,7},{7,5},{8,10},{10,8},{12,... | collective-permute-start | bytes 2359304 | tf_op jit(solution)/shard_map/ppermute | solution.py:455
  19.8 16.6 %collective-permute-start.1 = (bf16[768,512]{1,0:T(8,128)(2,1)}, bf16[768,512]{1,0:T(8,128)(2,1)S(1)}, u32[]{:S(2)}, u32[]{:S(2)}) collective-permute-start(bf16[768,512]{1,0:T(8,128)(2,1)} %constant_dynamic-update-slice_fusion), channel_id=1, source_target_pairs={{2,4},{4,2},{3,5},{5,3},{10,12},{12,10},{11,13},{13,11},{18,20},{2... | collective-permute-start | bytes 2359304 | tf_op jit(solution)/shard_map/ppermute | solution.py:454
  21.6 5.7 %copy-start.1 = (bf16[1,256,2048]{2,1,0:T(8,128)(2,1)S(1)}, bf16[1,256,2048]{2,1,0:T(8,128)(2,1)}, u32[]{:S(2)}) copy-start(bf16[1,256,2048]{2,1,0:T(8,128)(2,1)} %param.6) | copy-start | bytes 3145732
  36.5 21.7 %collective-permute-start.3 = (bf16[640,512]{1,0:T(8,128)(2,1)S(1)}, bf16[640,512]{1,0:T(8,128)(2,1)S(1)}, u32[]{:S(2)}, u32[]{:S(2)}) collective-permute-start(bf16[640,512]{1,0:T(8,128)(2,1)S(1)} %slice.31), channel_id=1, source_target_pairs={{2,0},{4,6},{3,1},{5,7},{10,8},{12,14},{11,9},{13,15},{18,16},{20,... | collective-permute-start | bytes 1966088 | tf_op jit(solution)/shard_map/ppermute | solution.py:469
  37.9 7.2 %collective-permute-start.6 = (bf16[512,256]{1,0:T(8,128)(2,1)S(1)}, bf16[512,256]{1,0:T(8,128)(2,1)S(1)}, u32[]{:S(2)}, u32[]{:S(2)}) collective-permute-start(bf16[512,256]{1,0:T(8,128)(2,1)S(1)} %pad_maximum_fusion.1), channel_id=1, source_target_pairs={{2,4},{4,2},{3,5},{5,3},{10,12},{12,10},{11,13},{13,11},{18,20},{2... | collective-permute-start | bytes 786440 | tf_op jit(solution)/shard_map/ppermute | solution.py:463
  38.7 8.8 %collective-permute-start.4 = (bf16[512,256]{1,0:T(8,128)(2,1)S(1)}, bf16[512,256]{1,0:T(8,128)(2,1)S(1)}, u32[]{:S(2)}, u32[]{:S(2)}) collective-permute-start(bf16[512,256]{1,0:T(8,128)(2,1)S(1)} %pad_maximum_fusion), channel_id=1, source_target_pairs={{2,4},{4,2},{3,5},{5,3},{10,12},{12,10},{11,13},{13,11},{18,20},{2... | collective-permute-start | bytes 786440 | tf_op jit(solution)/shard_map/ppermute | solution.py:463
  45.1 21.0 %collective-permute-start.7 = (bf16[512,256]{1,0:T(8,128)(2,1)S(1)}, bf16[512,256]{1,0:T(8,128)(2,1)S(1)}, u32[]{:S(2)}, u32[]{:S(2)}) collective-permute-start(bf16[512,256]{1,0:T(8,128)(2,1)S(1)} %collective-permute-done.6.refs_4_), channel_id=1, source_target_pairs={{2,0},{4,6},{3,1},{5,7},{10,8},{12,14},{11,9},{13,15},{18,16},{20,... | collective-permute-start | bytes 786440 | tf_op jit(solution)/shard_map/ppermute | solution.py:481
  47.4 23.9 %collective-permute-start.5 = (bf16[512,256]{1,0:T(8,128)(2,1)S(1)}, bf16[512,256]{1,0:T(8,128)(2,1)S(1)}, u32[]{:S(2)}, u32[]{:S(2)}) collective-permute-start(bf16[512,256]{1,0:T(8,128)(2,1)S(1)} %collective-permute-done.4.refs_4_), channel_id=1, source_target_pairs={{2,0},{4,6},{3,1},{5,7},{10,8},{12,14},{11,9},{13,15},{18,16},{20,... | collective-permute-start | bytes 786440 | tf_op jit(solution)/shard_map/ppermute | solution.py:481

commit v3 on v2

v3 whole, which is shorter than its diff:
```python
import functools
import math

import jax
import jax.numpy as jnp
from jax import lax
from jax.experimental import pallas as pl
from jax.experimental.pallas import tpu as pltpu
from jax.sharding import PartitionSpec as P

HD = 128
TILE = 32
TOGETHER = 4
LOW = -1e30
EXP_SCALE = math.log2(math.e) / math.sqrt(HD)
NT = (((1,), (1,)), ((), ()))
NN = (((1,), (0,)), ((), ()))


def mark_kernel(
    lengths_ref, images_ref, place_ref, marks_ref, row_start_ref, row_image_ref, *, samples, images
):
    tiles, _, height = row_start_ref.shape
    starts, total = [], jnp.int32(0)
    for j in range(samples):
        starts.append(total)
        total = total + lengths_ref[0, j]
    base = place_ref[0] * tiles * TILE
    for tile in range(tiles):
        first = base + tile * TILE
        row_t = first + (lax.broadcasted_iota(jnp.int32, (1, height), 1) & (TILE - 1))
        row_start = jnp.zeros((1, height), jnp.int32)
        row_image = jnp.zeros((1, height), jnp.int32)
        leading, low = jnp.int32(0), jnp.int32(0)
        met = [jnp.int32(0)] * images
        for j in range(samples):
            image = images_ref[0, j]
            row_start = jnp.where(row_t >= starts[j], starts[j], row_start)
            row_image = jnp.where(row_t >= starts[j], image, row_image)
            low = jnp.where(first >= starts[j], starts[j], low)
            leading = jnp.where(first >= starts[j], image, leading)
            inside = (starts[j] > first) & (starts[j] < first + TILE)
            met = [jnp.where(inside & (image == i), 1, m) for i, m in enumerate(met)]
        row_start_ref[tile] = row_start
        row_image_ref[tile] = row_image
        marks_ref[tile, 0] = low
        marks_ref[tile, 1] = leading
        for i in range(images):
            marks_ref[tile, 2 + i] = jnp.where(leading == i, 0, met[i])


def stacked_queries(q_ref, tile, g, group):
    first = g * group
    rows = pl.ds(tile * TILE, TILE)
    return jnp.concatenate(
        [q_ref[rows, (first + h) * HD : (first + h + 1) * HD] for h in range(group)], axis=0
    )


def write_heads(out_ref, mixed, total, tile, g, group):
    rows = (mixed * (1.0 / total)).T.astype(out_ref.dtype)
    for h in range(group):
        at = (g * group + h) * HD
        out_ref[pl.ds(tile * TILE, TILE), at : at + HD] = rows[h * TILE : (h + 1) * TILE]


def scores_of(keys, q):
    return lax.dot_general(keys, q, NT, preferred_element_type=jnp.float32)


def absorb(state, s, v):
    if state is None:
        new_top = jnp.max(s, axis=0, keepdims=True)
    else:
        top, total, mixed = state
        new_top = jnp.maximum(top, jnp.max(s, axis=0, keepdims=True))
    w = jnp.exp2((s - new_top) * EXP_SCALE)
    added = jnp.sum(w, axis=0, keepdims=True)
    product = lax.dot_general(v, w.astype(jnp.bfloat16), NN, preferred_element_type=jnp.float32)
    if state is None:
        return new_top, added, product
    decay = jnp.exp2((top - new_top) * EXP_SCALE)
    return new_top, total * decay + added, mixed * decay + product


def staggered(units, score, finish):
    waiting = None
    for unit in units:
        s = score(*unit)
        if waiting is not None:
            finish(*waiting)
        waiting = (*unit, s)
    finish(*waiting)


def lay(keys_at, flipped_at, ref, rows, kv_heads, g):
    keys_at[...] = ref[rows, g * HD : (g + 1) * HD]
    flipped_at[...] = ref[rows, (kv_heads + g) * HD : (kv_heads + g + 1) * HD].T


def self_kernel(
    marks_ref, place_ref, row_start_ref, q_ref, *refs, kv_heads, group, spans, parts, begin, end
):
    refs = list(refs)
    take = lambda n: [refs.pop(0) for _ in range(n)]
    pieces = take(len({part[1] for part in parts}))
    stat_in, mixed_in = (None, None) if begin else take(2)
    out_ref = take(1)[0] if end else None
    stat_ref, mixed_ref, keys_ref, flipped_ref = take(4)
    rows_here = q_ref.shape[0]
    tiles = rows_here // TILE
    height = group * TILE
    base = place_ref[0] * rows_here
    ats = [sum(count for _, count in spans[:n]) for n in range(len(spans))]

    lows = [marks_ref[tile, 0] for tile in range(tiles)]

    def limits(number):
        back, count = spans[number]
        past = base - (back - 1) * rows_here
        return past - count, past

    def reached(number):
        start, past = limits(number)
        many = jnp.int32(0)
        for low in lows:
            many = many + (low < past).astype(jnp.int32)
        return jnp.where(start >= 0, many, 0)

    counts = [reached(number) for number in range(len(spans))]
    for number, source, at, offset, count, only in parts:

        def fill(number=number, source=source, at=at, offset=offset, count=count):
            here = slice(ats[number] + offset, ats[number] + offset + count)
            for g in range(kv_heads):
                lay(
                    keys_ref.at[g, here], flipped_ref.at[g, :, here], pieces[source],
                    slice(at, at + count), kv_heads, g,
                )

        if spans[number][0] == 0:
            fill()
        else:
            asked = counts[number] > 0
            if only is not None:
                asked = asked & (place_ref[0] == only)
            pl.when(asked)(fill)

    def keep(tile, g, state):
        stat_ref[tile, g, 0:1, :] = state[0]
        stat_ref[tile, g, 1:2, :] = state[1]
        mixed_ref[tile, g] = state[2]

    def own_count(tile):
        return min(rows_here, -(-(tile + 1) * TILE // HD) * HD)

    def own_scores(tile, g):
        q = stacked_queries(q_ref, tile, g, group)
        return scores_of(keys_ref[g, : own_count(tile)], q)

    def own_finish(tile, g, s):
        row_start = row_start_ref[tile]
        row_t = base + tile * TILE
        row_t = row_t + (lax.broadcasted_iota(jnp.int32, (1, height), 1) & (TILE - 1))
        key_t = base + lax.broadcasted_iota(jnp.int32, (own_count(tile), 1), 0)
        s = jnp.where((key_t >= row_start) & (key_t <= row_t), s, LOW)
        keep(tile, g, absorb(None, s, flipped_ref[g, :, : own_count(tile)]))

    if begin:
        staggered(
            [(tile, g) for tile in range(tiles) for g in range(kv_heads)], own_scores, own_finish
        )
    else:
        stat_ref[...] = stat_in[...]
        mixed_ref[...] = mixed_in[...]

    together = math.gcd(tiles, TOGETHER)
    for number in range(1 if begin else 0, len(spans)):
        start, _ = limits(number)
        at, count = ats[number], spans[number][1]

        @pl.loop(0, (counts[number] + together - 1) // together)
        def _(turn, start=start, at=at, count=count):
            def scores(n, g):
                q = stacked_queries(q_ref, turn * together + n, g, group)
                return scores_of(keys_ref[g, at : at + count], q)

            def finish(n, g, s):
                tile = turn * together + n
                row_start = row_start_ref[tile]
                key_t = start + lax.broadcasted_iota(jnp.int32, (count, 1), 0)
                s = jnp.where(key_t >= row_start, s, LOW)
                old = stat_ref[tile, g, 0:1, :], stat_ref[tile, g, 1:2, :], mixed_ref[tile, g]
                keep(tile, g, absorb(old, s, flipped_ref[g, :, at : at + count]))

            staggered(
                [(n, g) for n in range(together) for g in range(kv_heads)], scores, finish
            )

    for tile in range(tiles if end else 0):
        for g in range(kv_heads):
            write_heads(out_ref, mixed_ref[tile, g], stat_ref[tile, g, 1:2, :], tile, g, group)


def cross_kernel(
    marks_ref, place_ref, row_image_ref, q_ref, *refs, kv_heads, group, heads, sources, begin, end
):
    refs = list(refs)
    take = lambda n: [refs.pop(0) for _ in range(n)]
    pieces = [take(len(source)) for source in sources]
    stat_in, mixed_in = (None, None) if begin else take(2)
    rest_ref = take(1)[0] if end and heads[0] > 0 else None
    out_ref = take(1)[0] if end else None
    stat_ref, mixed_ref, keys_ref, flipped_ref = take(4)
    tiles = q_ref.shape[0] // TILE
    image_count = keys_ref.shape[0]

    def fill(ref, at, parts, each):
        held = ref.shape[1] // HD // 2
        for n, g in enumerate(heads):
            k_at = (g if held == kv_heads else n) * HD
            v_at = k_at + held * HD
            for image in range(image_count):
                values = []
                for part in range(parts):
                    row = (part * image_count + image) * each
                    here = slice(at + part * each, at + (part + 1) * each)
                    keys_ref[image, n, here] = ref[row : row + each, k_at : k_at + HD]
                    values.append(ref[row : row + each, v_at : v_at + HD])
                whole = jnp.concatenate(values, axis=0)
                flipped_ref[image, n, :, at : at + parts * each] = whole.T

    at = 0
    for source, given in zip(sources, pieces):
        for number, ((parts, each), ref) in enumerate(zip(source, given)):
            put = functools.partial(fill, ref, at, parts, each)
            if len(source) == 1:
                put()
            else:
                pl.when(place_ref[1] == 1 - number)(put)
        at += source[0][0] * source[0][1]

    def keep(tile, n, state):
        stat_ref[tile, n, 0:1, :] = state[0]
        stat_ref[tile, n, 1:2, :] = state[1]
        mixed_ref[tile, n] = state[2]

    def chosen(mine, new, old):
        if old is None:
            old = LOW, 0.0, 0.0
        return [jnp.where(mine, n, o) for n, o in zip(new, old)]

    def scores(tile, n):
        q = stacked_queries(q_ref, tile, heads[n], group)
        return scores_of(keys_ref[marks_ref[tile, 1], n], q)

    def finish(tile, n, s):
        leading = marks_ref[tile, 1]
        old, g = None, heads[n]
        if not begin:
            old = stat_in[tile, g, 0:1, :], stat_in[tile, g, 1:2, :], mixed_in[tile, g]
        new = absorb(old, s, flipped_ref[leading, n])
        keep(tile, n, chosen(row_image_ref[tile] == leading, new, old))

    order = range(len(heads))
    staggered([(tile, n) for tile in range(tiles) for n in order], scores, finish)

    @pl.loop(0, tiles)
    def _(tile):
        for image in range(image_count):

            @pl.when(marks_ref[tile, 2 + image] == 1)
            def _(image=image):
                mine = row_image_ref[tile] == image
                olds = [
                    (stat_ref[tile, n, 0:1, :], stat_ref[tile, n, 1:2, :], mixed_ref[tile, n])
                    for n in order
                ]
                ss = [
                    scores_of(keys_ref[image, n], stacked_queries(q_ref, tile, heads[n], group))
                    for n in order
                ]
                for n in order:
                    new = absorb(olds[n], ss[n], flipped_ref[image, n])
                    keep(tile, n, chosen(mine, new, olds[n]))

    if rest_ref is not None:
        out_ref[:, : rest_ref.shape[1]] = rest_ref[...]
    for tile in range(tiles if end else 0):
        for n in order:
            write_heads(
                out_ref, mixed_ref[tile, n], stat_ref[tile, n, 1:2, :], tile, heads[n], group
            )


def smem():
    return pl.BlockSpec(memory_space=pltpu.SMEM)


def vmem():
    return pl.BlockSpec(memory_space=pltpu.VMEM)


def cost(rows, width, keys):
    return pl.CostEstimate(
        flops=8 * rows * width * keys, bytes_accessed=4 * rows * width,
        transcendentals=rows * (width // HD) * keys,
    )


def state_shapes(rows, kv_heads, group):
    tiles, height = rows // TILE, group * TILE
    return (tiles, kv_heads, 8, height), (tiles, kv_heads, HD, height)


def state_call(kernel, operands, rows, width, keys, shapes, scratch, end, dtype):
    state_scratch = []
    if end:
        out_shape = jax.ShapeDtypeStruct((rows, width), dtype)
        state_scratch = [pltpu.VMEM(s, jnp.float32) for s in shapes]
    else:
        out_shape = [jax.ShapeDtypeStruct(s, jnp.float32) for s in shapes]
    return pl.pallas_call(
        kernel,
        out_shape=out_shape,
        in_specs=[smem()] * 2 + [vmem()] * (len(operands) - 2),
        out_specs=vmem() if end else [vmem(), vmem()],
        scratch_shapes=state_scratch + scratch,
        compiler_params=pltpu.CompilerParams(vmem_limit_bytes=28 << 20),
        cost_estimate=cost(rows, width, keys),
    )(*operands)


def marks_of(lengths, images, place, rows, group, image_count):
    tiles, height = rows // TILE, group * TILE
    row_shape = jax.ShapeDtypeStruct((tiles, 1, height), jnp.int32)
    return pl.pallas_call(
        functools.partial(mark_kernel, samples=lengths.shape[1], images=image_count),
        out_shape=[jax.ShapeDtypeStruct((tiles, 2 + image_count), jnp.int32), row_shape, row_shape],
        in_specs=[smem()] * 3,
        out_specs=[smem(), vmem(), vmem()],
    )(lengths, images, place)


def self_attention(marks, place, row_start, q, pieces, spans, parts, state, end, kv_heads, group):
    rows, width = q.shape
    keys = sum(count for _, count in spans)
    begin = state is None
    kernel = functools.partial(
        self_kernel, kv_heads=kv_heads, group=group, spans=spans, parts=parts,
        begin=begin, end=end,
    )
    scratch = [
        pltpu.VMEM((kv_heads, keys, HD), q.dtype), pltpu.VMEM((kv_heads, HD, keys), q.dtype)
    ]
    operands = (marks, place, row_start, q, *pieces, *(() if begin else state))
    shapes = state_shapes(rows, kv_heads, group)
    return state_call(kernel, operands, rows, width, keys, shapes, scratch, end, q.dtype)


def cross_attention(
    marks, place, row_image, q, sources, state, end, kv_heads, group, image_count,
    heads=None, rest=None,
):
    heads = tuple(range(kv_heads)) if heads is None else heads
    rows, width = q.shape
    begin = state is None
    kernel = functools.partial(
        cross_kernel, kv_heads=kv_heads, group=group, heads=heads,
        sources=tuple(tuple(piece[1:] for piece in source) for source in sources),
        begin=begin, end=end,
    )
    pieces = [piece[0] for source in sources for piece in source]
    keys = sum(source[0][1] * source[0][2] for source in sources)
    scratch = [
        pltpu.VMEM((image_count, len(heads), keys, HD), q.dtype),
        pltpu.VMEM((image_count, len(heads), HD, keys), q.dtype),
    ]
    operands = (marks, place, row_image, q, *pieces, *(() if begin else state))
    if rest is not None:
        operands += (rest,)
    shapes = state_shapes(rows, len(heads), group)
    width = (heads[-1] + 1) * group * HD
    return state_call(kernel, operands, rows, width, keys, shapes, scratch, end, q.dtype)


def per_device(q_self, kv_self, q_cross, kv_cross, sample_lengths, sample_image, *, n_pipe, n_ctx):
    rows = q_self.shape[1]
    kv_heads = kv_self.shape[3] // HD
    group = q_self.shape[2] // HD // kv_heads
    image_count, each = kv_cross.shape[1:3]
    z = lax.axis_index("ctx")
    inner = ((z == 1) | (z == 2)).astype(jnp.int32)
    place = jnp.stack([z, inner]).astype(jnp.int32)

    shift = lambda piece, step: lax.ppermute(
        piece, "ctx", [(c, c + 1) for c in range(step - 1, n_ctx - 1)]
    )
    passed = shift(kv_self[0], 1)
    arrived = lax.all_to_all(kv_cross, "pipe", split_axis=0, concat_axis=0, tiled=True)
    own = kv_self[0].reshape(rows, -1)

    marks, row_start, row_image = marks_of(
        sample_lengths, sample_image, place, rows, group, image_count
    )
    attend_self = functools.partial(
        self_attention, marks, place, row_start, q_self[0], kv_heads=kv_heads, group=group
    )
    attend_cross = functools.partial(
        cross_attention, marks, place, row_image, q_cross[0],
        kv_heads=kv_heads, group=group, image_count=image_count,
    )
    if n_ctx == 4:
        at = lambda array: (array, n_pipe, each)
        self_state = attend_self([own], ((0, rows),), ((0, 0, 0, 0, rows, None),), None, False)
        arrived, passed, self_state = lax.optimization_barrier((arrived, passed, self_state))
        own_rows = arrived.reshape(-1, own.shape[1])

        near = lax.ppermute(own_rows, "ctx", [(1, 2), (2, 1)])
        pair = lax.ppermute(own_rows, "ctx", [(0, 1), (1, 0), (2, 3), (3, 2)])
        state = attend_cross([[at(own_rows)]], None, False)
        passed, state = lax.optimization_barrier((passed, state))
        half = rows // 2
        two_back = lax.ppermute(passed, "ctx", [(1, 2), (2, 3)]).reshape(rows, -1)
        three_back = lax.ppermute(passed[half:], "ctx", [(1, 3)]).reshape(half, -1)
        self_state = attend_self(
            [passed.reshape(rows, -1)], ((1, rows),), ((0, 0, 0, 0, rows, None),), self_state, False
        )
        near, pair, self_state = lax.optimization_barrier((near, pair, self_state))

        near_on = lax.ppermute(near, "ctx", [(1, 0), (2, 3)])
        columns = lambda j: pair[:, j * HD : (j + 1) * HD]
        far = [
            lax.ppermute(
                jnp.concatenate([columns(g), columns(kv_heads + g)], axis=1),
                "ctx", [(1, 2), (2, 1)],
            )
            for g in range(kv_heads)
        ]
        state = attend_cross([[at(pair)]], state, False)
        far[0], state = lax.optimization_barrier((far[0], state))
        self_out = attend_self(
            [two_back, three_back], ((2, rows), (3, half)),
            ((0, 0, 0, 0, rows, None), (1, 1, 0, 0, half, 3)), self_state, True,
        )
        far[-1], self_out = lax.optimization_barrier((far[-1], self_out))
        far_on = [lax.ppermute(part, "ctx", [(1, 0), (2, 3)]) for part in far]
        state = attend_cross([[at(near), at(near_on)]], state, False)
        cross_out = None
        for g in range(kv_heads):
            cross_out = attend_cross(
                [[at(far[g]), at(far_on[g])]], state, True, heads=(g,), rest=cross_out
            )
    else:
        longest = rows * n_ctx * 5 // 8
        pieces, spans = [own, passed.reshape(rows, -1)], [(0, rows), (1, rows)]
        left, step = longest - 1 - rows, 1
        while left > 0 and step < n_ctx - 1:
            step += 1
            count = min(rows, -(-left // HD) * HD)
            pieces.append(shift(pieces[-1][rows - count :], step))
            spans.append((step, count))
            left -= rows
        parts = tuple((n, n, 0, 0, count, None) for n, (_, count) in enumerate(spans))
        self_out = attend_self(pieces, tuple(spans), parts, None, True)
        own_rows = arrived.reshape(-1, own.shape[1])
        gathered = lax.all_gather(own_rows, "ctx", axis=0, tiled=True)
        cross_out = attend_cross([[(gathered, n_ctx * n_pipe, each)]], None, True)
    return self_out[None], cross_out[None]


def solution(mesh):
    in_specs = (
        P("pipe", "ctx", "tp"),
        P("pipe", "ctx", None, "tp"),
        P("pipe", "ctx", "tp"),
        P(None, None, ("pipe", "ctx"), None, "tp"),
        P("pipe", None),
        P("pipe", None),
    )
    out_specs = (P("pipe", "ctx", "tp"), P("pipe", "ctx", "tp"))
    body = functools.partial(
        per_device, n_pipe=mesh.shape["pipe"], n_ctx=mesh.shape["ctx"]
    )
    return jax.shard_map(
        body, mesh=mesh, in_specs=in_specs, out_specs=out_specs, check_vma=False
    )
```

time: 75.6 us -> 75.6 us (level)
  the two profiles are of different devices: /device:TPU:0 before, /device:TPU:20 now
where the time goes in v3:
time: 75.6 us; the launch traced here: 75.4 us
  starting transfers between devices  32.9 us (44%)
  Pallas kernels  32.4 us (43%)
  local copies, waits for them, and re-layouts  7.44 us (10%)
  waiting for transfers between devices  0.99 us (1%)
  between operations  0.97 us (1%)
    pallas_call x8, Pallas kernels, state_call(): pl.pallas_call(kernel, out_shape=out_shape, in_specs=[smem()] * 2 + [vmem...  30.8 us
    ppermute x2, starting transfers between devices, per_device(): far_on = [lax.ppermute(part, 'ctx', [(1, 0), (2, 3)]) for part in far]  9.56 us
    ppermute x2, starting transfers between devices, per_device(): lax.ppermute(jnp.concatenate([columns(g), columns(kv_heads + g)], axis=1)...  6.47 us
    unnamed x25, local copies, waits for them, and re-layouts  6.35 us
    all_to_all x1, starting transfers between devices, per_device(): lax.all_to_all(kv_cross, 'pipe', split_axis=0, concat_axis=0, tiled=True)  4.63 us
    ppermute x1, starting transfers between devices, per_device(): two_back = lax.ppermute(passed, 'ctx', [(1, 2), (2, 3)]).reshape(rows, -1)  4.39 us
    ppermute x1, starting transfers between devices, per_device(): lax.ppermute(piece, 'ctx', [(c, c + 1) for c in range(step - 1, n_ctx - 1)])  3.47 us
    ppermute x1, starting transfers between devices, per_device(): near = lax.ppermute(own_rows, 'ctx', [(1, 2), (2, 1)])  2.36 us
  transfers between devices with their start and end apart: 11, of which 1 were waited for; matrix products, arithmetic and copies ran while one was open for 5% of the time, Pallas kernels for 38%

profile of v3, /device:TPU:20, one launch (start us, length us, event | category | flops | bytes accessed | tf_op | source)
XLA Modules:
  0.0 75.4 jit_solution(14268480670700625247)
XLA Ops:
  0.6 4.6 %all-to-all-start = ((bf16[4,2,64,2,256]{4,3,2,1,0:T(2,128)(2,1)}), bf16[4,2,64,2,256]{4,3,2,1,0:T(2,128)(2,1)}, u32[]{:S(2)}, u32[]{:S(2)}) async-start(bf16[4,2,64,2,256]{4,3,2,1,0:T(2,128)(2,1)} %param.9), calls=%async_computation | async-start | bytes 1048576 | tf_op jit(solution)/shard_map/all_to_all | solution.py:400
  5.3 3.5 %collective-permute-start = (bf16[256,2,256]{2,1,0:T(2,128)(2,1)}, bf16[256,2,256]{2,1,0:T(2,128)(2,1)}, u32[]{:S(2)}, u32[]{:S(2)}) collective-permute-start(bf16[256,2,256]{2,1,0:T(2,128)(2,1)} %bitcast.35), channel_id=1, source_target_pairs={{0,2},{2,4},{4,6},{1,3},{3,5},{5,7},{8,10},{10,12},{12,14},{9,11},... | collective-permute-start | bytes 786440 | tf_op jit(solution)/shard_map/ppermute | solution.py:396
  8.8 1.0 %copy.8 = bf16[32,8,2,256]{3,1,2,0:T(8,128)(2,1)S(1)} copy(bf16[32,8,2,256]{3,2,1,0:T(2,128)(2,1)} %bitcast.36) | data formatting | bytes 524288
  9.7 0.6 pad_add_fusion.place_ref
  10.3 1.6 %shard_map.77 = (s32[8,4]{1,0:T(8,128)}, s32[8,1,256]{2,1,0:T(1,128)}, s32[8,1,256]{2,1,0:T(1,128)}) custom-call(s32[1,8]{1,0:T(1,128)} %lengths_ref.1, s32[1,8]{1,0:T(1,128)} %images_ref.1, s32[2]{0:T(128)} %pad_add_fusion.place_ref), custom_call_target="tpu_custom_call" | custom-call | tf_op jit(solution)/shard_map/pallas_call | solution.py:337
  11.9 0.0 copy-start.2
  11.9 0.7 copy-done.2
  12.6 0.6 copy-done.4
  13.2 1.2 %copy-done.6 = bf16[1,256,2048]{2,1,0:T(8,128)(2,1)S(1)} copy-done((bf16[1,256,2048]{2,1,0:T(8,128)(2,1)S(1)}, bf16[1,256,2048]{2,1,0:T(8,128)(2,1)}, u32[]{:S(2)}) %copy-start.6) | copy-done | bytes 1048600
  14.4 0.7 copy-done.8
  15.1 2.6 %shard_map.78 = (f32[8,2,8,256]{3,2,1,0:T(8,128)S(1)}, f32[8,2,128,256]{3,2,1,0:T(8,128)S(1)}) custom-call(s32[8,4]{1,0:T(8,128)S(1)} %copy-done.2, s32[2]{0:T(128)S(1)} %copy-done.4, s32[8,1,256]{2,1,0:T(1,128)S(1)} %copy-done.8, bf16[256,2048]{1,0:T(8,128)(2,1)S(1)} %bitcast.31, bf16[256,512]{1,0:T(8,128)(2,1)S(1)} %bitcast.28), custom_call_target="tpu_custom_call" | custom-call | flops 1073741824 | bytes 2097152 | tf_op jit(solution)/shard_map/pallas_call | solution.py:323
  17.7 0.0 collective-permute-done
  17.7 0.0 all-to-all-done
  17.7 1.1 %copy.9 = bf16[64,8,2,256]{3,1,2,0:T(8,128)(2,1)S(1)} copy(bf16[64,8,2,256]{3,2,1,0:T(2,128)(2,1)} %bitcast.11) | data formatting | bytes 1048576
  18.9 2.4 %collective-permute-start.1 = (bf16[512,512]{1,0:T(8,128)(2,1)S(1)}, bf16[512,512]{1,0:T(8,128)(2,1)S(1)}, u32[]{:S(2)}, u32[]{:S(2)}) collective-permute-start(bf16[512,512]{1,0:T(8,128)(2,1)S(1)} %bitcast.24), channel_id=1, source_target_pairs={{2,4},{4,2},{3,5},{5,3},{10,12},{12,10},{11,13},{13,11},{18,20},{2... | collective-permute-start | bytes 1572872 | tf_op jit(solution)/shard_map/ppermute | solution.py:419
  21.2 0.1 collective-permute-start.2
  21.3 0.0 copy-done
  21.3 0.0 copy-done.1
  21.4 0.0 copy-start.7
  21.4 0.0 copy-start.9
  21.4 4.0 %shard_map.79 = (f32[8,2,8,256]{3,2,1,0:T(8,128)S(1)}, f32[8,2,128,256]{3,2,1,0:T(8,128)S(1)}) custom-call(s32[8,4]{1,0:T(8,128)S(1)} %copy-done.3, s32[2]{0:T(128)S(1)} %copy-done.5, s32[8,1,256]{2,1,0:T(1,128)S(1)} %copy-done.1, bf16[256,2048]{1,0:T(8,128)(2,1)S(1)} %bitcast.19, bf16[512,512]{1,0:T(8,128)(2,1)S(1)} %bitcast.26), custom_call_target="tpu_custom_call" | custom-call | flops 1073741824 | bytes 2097152 | tf_op jit(solution)/shard_map/pallas_call | solution.py:323
  25.4 4.4 %collective-permute-start.4 = (bf16[256,2,256]{2,1,0:T(2,128)(2,1)}, bf16[256,2,256]{2,1,0:T(2,128)(2,1)S(1)}, u32[]{:S(2)}, u32[]{:S(2)}) collective-permute-start(bf16[256,2,256]{2,1,0:T(2,128)(2,1)} %collective-permute-done), channel_id=1, source_target_pairs={{2,4},{4,6},{3,5},{5,7},{10,12},{12,14},{11,13},{13,15},{18,20},{2... | collective-permute-start | bytes 786440 | tf_op jit(solution)/shard_map/ppermute | solution.py:424
  29.8 1.0 %copy.10 = bf16[32,8,2,256]{3,1,2,0:T(8,128)(2,1)S(1)} copy(bf16[32,8,2,256]{3,2,1,0:T(2,128)(2,1)} %bitcast.13) | data formatting | bytes 524288
  30.8 0.0 copy-done.7
  30.8 0.0 copy-done.9
  30.8 3.8 %shard_map.80 = (f32[8,2,8,256]{3,2,1,0:T(8,128)S(1)}, f32[8,2,128,256]{3,2,1,0:T(8,128)S(1)}) custom-call(s32[8,4]{1,0:T(8,128)S(1)} %copy-done.3, s32[2]{0:T(128)S(1)} %copy-done.5, s32[8,1,256]{2,1,0:T(1,128)S(1)} %copy-done.9, bf16[256,2048]{1,0:T(8,128)(2,1)S(1)} %bitcast.32, bf16[256,512]{1,0:T(8,128)(2,1)S(1)} %bitcast.29, ...), custom_call_target="tpu_custom_call" | custom-call | flops 1073741824 | bytes 2097152 | tf_op jit(solution)/shard_map/pallas_call | solution.py:323
  34.7 1.0 %collective-permute-done.1.refs_0_ = bf16[512,512]{1,0:T(8,128)(2,1)S(1)} collective-permute-done((bf16[512,512]{1,0:T(8,128)(2,1)S(1)}, bf16[512,512]{1,0:T(8,128)(2,1)S(1)}, u32[]{:S(2)}, u32[]{:S(2)}) %collective-permute-start.1) | collective-permute-done | bytes 524320 | tf_op jit(solution)/shard_map/ppermute | solution.py:419
  35.6 0.0 collective-permute-done.2.refs_0_
  35.6 0.1 fusion
  35.8 2.0 %collective-permute-start.8 = (bf16[512,256]{1,0:T(8,128)(2,1)S(1)}, bf16[512,256]{1,0:T(8,128)(2,1)S(1)}, u32[]{:S(2)}, u32[]{:S(2)}) collective-permute-start(bf16[512,256]{1,0:T(8,128)(2,1)S(1)} %pad_maximum_fusion.1), channel_id=1, source_target_pairs={{2,4},{4,2},{3,5},{5,3},{10,12},{12,10},{11,13},{13,11},{18,20},{2... | collective-permute-start | bytes 786440 | tf_op jit(solution)/shard_map/ppermute | solution.py:434
  37.8 1.3 %collective-permute-start.7 = (bf16[512,512]{1,0:T(8,128)(2,1)S(1)}, bf16[512,512]{1,0:T(8,128)(2,1)S(1)}, u32[]{:S(2)}, u32[]{:S(2)}) collective-permute-start(bf16[512,512]{1,0:T(8,128)(2,1)S(1)} %collective-permute-done.1.refs_0_), channel_id=1, source_target_pairs={{2,0},{4,6},{3,1},{5,7},{10,8},{12,14},{11,9},{13,15},{18,16},{20,... | collective-permute-start | bytes 1572872 | tf_op jit(solution)/shard_map/ppermute | solution.py:431
  39.1 1.0 %slice.17 = bf16[128,2,256]{2,1,0:T(2,128)(2,1)S(1)} slice(bf16[256,2,256]{2,1,0:T(2,128)(2,1)} %collective-permute-done), slice={[128:256], [0:2], [0:256]} | slice | bytes 262144 | tf_op jit(solution)/shard_map/slice | solution.py:425
  40.1 0.7 collective-permute-start.5
  40.8 4.5 %collective-permute-start.3 = (bf16[512,256]{1,0:T(8,128)(2,1)S(1)}, bf16[512,256]{1,0:T(8,128)(2,1)S(1)}, u32[]{:S(2)}, u32[]{:S(2)}) collective-permute-start(bf16[512,256]{1,0:T(8,128)(2,1)S(1)} %pad_maximum_fusion), channel_id=1, source_target_pairs={{2,4},{4,2},{3,5},{5,3},{10,12},{12,10},{11,13},{13,11},{18,20},{2... | collective-permute-start | bytes 786440 | tf_op jit(solution)/shard_map/ppermute | solution.py:434
  45.3 0.0 collective-permute-done.5
  45.3 0.0 collective-permute-done.4
  45.4 4.0 %shard_map.82 = (f32[8,2,8,256]{3,2,1,0:T(8,128)S(1)}, f32[8,2,128,256]{3,2,1,0:T(8,128)S(1)}) custom-call(s32[8,4]{1,0:T(8,128)S(1)} %copy-done.3, s32[2]{0:T(128)S(1)} %copy-done.5, s32[8,1,256]{2,1,0:T(1,128)S(1)} %copy-done.1, bf16[256,2048]{1,0:T(8,128)(2,1)S(1)} %bitcast.20, bf16[512,512]{1,0:T(8,128)(2,1)S(1)} %collective-permute-done.2.refs_0_, ...), custom_call_target="tpu_custom_call" | custom-call | flops 1073741824 | bytes 2097152 | tf_op jit(solution)/shard_map/pallas_call | solution.py:323
  49.4 0.0 collective-permute-done.8.refs_0_
  49.4 8.3 %collective-permute-start.9 = (bf16[512,256]{1,0:T(8,128)(2,1)S(1)}, bf16[512,256]{1,0:T(8,128)(2,1)S(1)}, u32[]{:S(2)}, u32[]{:S(2)}) collective-permute-start(bf16[512,256]{1,0:T(8,128)(2,1)S(1)} %collective-permute-done.8.refs_0_), channel_id=1, source_target_pairs={{2,0},{4,6},{3,1},{5,7},{10,8},{12,14},{11,9},{13,15},{18,16},{20,... | collective-permute-start | bytes 786440 | tf_op jit(solution)/shard_map/ppermute | solution.py:447
  57.7 5.3 %shard_map.81 = bf16[256,2048]{1,0:T(8,128)(2,1)} custom-call(s32[8,4]{1,0:T(8,128)S(1)} %copy-done.3, s32[2]{0:T(128)S(1)} %copy-done.5, s32[8,1,256]{2,1,0:T(1,128)S(1)} %copy-done.9, bf16[256,2048]{1,0:T(8,128)(2,1)S(1)} %bitcast.33, bf16[256,512]{1,0:T(8,128)(2,1)S(1)} %bitcast.27, bf16[128,512]{1,0:T(8,128)(2,1)S(1)} %bitcast.30, ...), custom_call_target="tpu_custom_call" | custom-call | flops 1610612736 | bytes 2097152 | tf_op jit(solution)/shard_map/pallas_call | solution.py:323
  63.0 0.0 collective-permute-done.3.refs_0_
  63.0 1.3 %collective-permute-start.6 = (bf16[512,256]{1,0:T(8,128)(2,1)S(1)}, bf16[512,256]{1,0:T(8,128)(2,1)S(1)}, u32[]{:S(2)}, u32[]{:S(2)}) collective-permute-start(bf16[512,256]{1,0:T(8,128)(2,1)S(1)} %collective-permute-done.3.refs_0_), channel_id=1, source_target_pairs={{2,0},{4,6},{3,1},{5,7},{10,8},{12,14},{11,9},{13,15},{18,16},{20,... | collective-permute-start | bytes 786440 | tf_op jit(solution)/shard_map/ppermute | solution.py:447
  64.3 0.0 collective-permute-done.7.refs_1_
  64.4 4.1 %shard_map.83 = (f32[8,2,8,256]{3,2,1,0:T(8,128)S(1)}, f32[8,2,128,256]{3,2,1,0:T(8,128)S(1)}) custom-call(s32[8,4]{1,0:T(8,128)S(1)} %copy-done.3, s32[2]{0:T(128)S(1)} %copy-done.5, s32[8,1,256]{2,1,0:T(1,128)S(1)} %copy-done.1, bf16[256,2048]{1,0:T(8,128)(2,1)S(1)} %bitcast.21, bf16[512,512]{1,0:T(8,128)(2,1)S(1)} %collective-permute-done.1.refs_0_, ...), custom_call_target="tpu_custom_call" | custom-call | flops 1073741824 | bytes 2097152 | tf_op jit(solution)/shard_map/pallas_call | solution.py:323
  68.5 0.0 collective-permute-done.9.refs_1_
  68.5 2.9 %shard_map.84.refs_4_ = bf16[256,1024]{1,0:T(8,128)(2,1)S(1)} custom-call(s32[8,4]{1,0:T(8,128)S(1)} %copy-done.3, s32[2]{0:T(128)S(1)} %copy-done.5, s32[8,1,256]{2,1,0:T(1,128)S(1)} %copy-done.1, bf16[256,2048]{1,0:T(8,128)(2,1)S(1)} %bitcast.22, bf16[512,256]{1,0:T(8,128)(2,1)S(1)} %collective-permute-done.8.refs_0_, ...), custom_call_target="tpu_custom_call" | custom-call | flops 536870912 | bytes 1048576 | tf_op jit(solution)/shard_map/pallas_call | solution.py:323
  71.4 0.0 collective-permute-done.6.refs_1_
  71.5 3.9 %shard_map.85 = bf16[256,2048]{1,0:T(8,128)(2,1)} custom-call(s32[8,4]{1,0:T(8,128)S(1)} %copy-done.3, s32[2]{0:T(128)S(1)} %copy-done.5, s32[8,1,256]{2,1,0:T(1,128)S(1)} %copy-done.1, bf16[256,2048]{1,0:T(8,128)(2,1)S(1)} %bitcast.23, bf16[512,256]{1,0:T(8,128)(2,1)S(1)} %collective-permute-done.3.refs_0_, ...), custom_call_target="tpu_custom_call" | custom-call | flops 1073741824 | bytes 2097152 | tf_op jit(solution)/shard_map/pallas_call | solution.py:323
  (13 shorter events, 0.1 us)
Async XLA Ops:
  0.6 17.1 %all-to-all-start = ((bf16[4,2,64,2,256]{4,3,2,1,0:T(2,128)(2,1)}), bf16[4,2,64,2,256]{4,3,2,1,0:T(2,128)(2,1)}, u32[]{:S(2)}, u32[]{:S(2)}) async-start(bf16[4,2,64,2,256]{4,3,2,1,0:T(2,128)(2,1)} %param.9), calls=%async_computation | async-start | bytes 1048576 | tf_op jit(solution)/shard_map/all_to_all | solution.py:400
  5.3 12.5 %collective-permute-start = (bf16[256,2,256]{2,1,0:T(2,128)(2,1)}, bf16[256,2,256]{2,1,0:T(2,128)(2,1)}, u32[]{:S(2)}, u32[]{:S(2)}) collective-permute-start(bf16[256,2,256]{2,1,0:T(2,128)(2,1)} %bitcast.35), channel_id=1, source_target_pairs={{0,2},{2,4},{4,6},{1,3},{3,5},{5,7},{8,10},{10,12},{12,14},{9,11},... | collective-permute-start | bytes 786440 | tf_op jit(solution)/shard_map/ppermute | solution.py:396
  11.9 0.7 copy-start.2
  12.6 0.6 copy-start.4
  13.2 1.2 %copy-start.6 = (bf16[1,256,2048]{2,1,0:T(8,128)(2,1)S(1)}, bf16[1,256,2048]{2,1,0:T(8,128)(2,1)}, u32[]{:S(2)}) copy-start(bf16[1,256,2048]{2,1,0:T(8,128)(2,1)} %param.6) | copy-start | bytes 3145732
  14.4 0.7 copy-start.8
  15.1 6.2 %copy-start = (bf16[1,256,2048]{2,1,0:T(8,128)(2,1)S(1)}, bf16[1,256,2048]{2,1,0:T(8,128)(2,1)}, u32[]{:S(2)}) copy-start(bf16[1,256,2048]{2,1,0:T(8,128)(2,1)} %param.8) | copy-start | bytes 3145732
  15.1 6.2 %copy-start.1 = (s32[8,1,256]{2,1,0:T(1,128)S(1)}, s32[8,1,256]{2,1,0:T(1,128)}, u32[]{:S(2)}) copy-start(s32[8,1,256]{2,1,0:T(1,128)} %get-tuple-element.37.row_image_ref) | copy-start | bytes 24580
  15.1 6.2 %copy-start.3 = (s32[8,4]{1,0:T(8,128)S(1)}, s32[8,4]{1,0:T(8,128)}, u32[]{:S(2)}) copy-start(s32[8,4]{1,0:T(8,128)} %get-tuple-element.31.marks_ref) | copy-start | bytes 388
  15.1 6.3 %copy-start.5 = (s32[2]{0:T(128)S(1)}, s32[2]{0:T(128)}, u32[]{:S(2)}) copy-start(s32[2]{0:T(128)} %pad_add_fusion.place_ref) | copy-start | bytes 28
  18.9 16.8 %collective-permute-start.1 = (bf16[512,512]{1,0:T(8,128)(2,1)S(1)}, bf16[512,512]{1,0:T(8,128)(2,1)S(1)}, u32[]{:S(2)}, u32[]{:S(2)}) collective-permute-start(bf16[512,512]{1,0:T(8,128)(2,1)S(1)} %bitcast.24), channel_id=1, source_target_pairs={{2,4},{4,2},{3,5},{5,3},{10,12},{12,10},{11,13},{13,11},{18,20},{2... | collective-permute-start | bytes 1572872 | tf_op jit(solution)/shard_map/ppermute | solution.py:419
  21.2 14.4 %collective-permute-start.2 = (bf16[512,512]{1,0:T(8,128)(2,1)S(1)}, bf16[512,512]{1,0:T(8,128)(2,1)S(1)}, u32[]{:S(2)}, u32[]{:S(2)}) collective-permute-start(bf16[512,512]{1,0:T(8,128)(2,1)S(1)} %bitcast.25), channel_id=1, source_target_pairs={{0,2},{2,0},{4,6},{6,4},{1,3},{3,1},{5,7},{7,5},{8,10},{10,8},{12,... | collective-permute-start | bytes 1572872 | tf_op jit(solution)/shard_map/ppermute | solution.py:420
  21.4 9.5 %copy-start.7 = (bf16[1,256,2048]{2,1,0:T(8,128)(2,1)S(1)}, bf16[1,256,2048]{2,1,0:T(8,128)(2,1)}, u32[]{:S(2)}) copy-start(bf16[1,256,2048]{2,1,0:T(8,128)(2,1)} %param.6) | copy-start | bytes 3145732
  21.4 9.5 %copy-start.9 = (s32[8,1,256]{2,1,0:T(1,128)S(1)}, s32[8,1,256]{2,1,0:T(1,128)}, u32[]{:S(2)}) copy-start(s32[8,1,256]{2,1,0:T(1,128)} %get-tuple-element.32.row_start_ref) | copy-start | bytes 24580
  25.4 19.9 %collective-permute-start.4 = (bf16[256,2,256]{2,1,0:T(2,128)(2,1)}, bf16[256,2,256]{2,1,0:T(2,128)(2,1)S(1)}, u32[]{:S(2)}, u32[]{:S(2)}) collective-permute-start(bf16[256,2,256]{2,1,0:T(2,128)(2,1)} %collective-permute-done), channel_id=1, source_target_pairs={{2,4},{4,6},{3,5},{5,7},{10,12},{12,14},{11,13},{13,15},{18,20},{2... | collective-permute-start | bytes 786440 | tf_op jit(solution)/shard_map/ppermute | solution.py:424
  35.8 13.7 %collective-permute-start.8 = (bf16[512,256]{1,0:T(8,128)(2,1)S(1)}, bf16[512,256]{1,0:T(8,128)(2,1)S(1)}, u32[]{:S(2)}, u32[]{:S(2)}) collective-permute-start(bf16[512,256]{1,0:T(8,128)(2,1)S(1)} %pad_maximum_fusion.1), channel_id=1, source_target_pairs={{2,4},{4,2},{3,5},{5,3},{10,12},{12,10},{11,13},{13,11},{18,20},{2... | collective-permute-start | bytes 786440 | tf_op jit(solution)/shard_map/ppermute | solution.py:434
  37.8 26.6 %collective-permute-start.7 = (bf16[512,512]{1,0:T(8,128)(2,1)S(1)}, bf16[512,512]{1,0:T(8,128)(2,1)S(1)}, u32[]{:S(2)}, u32[]{:S(2)}) collective-permute-start(bf16[512,512]{1,0:T(8,128)(2,1)S(1)} %collective-permute-done.1.refs_0_), channel_id=1, source_target_pairs={{2,0},{4,6},{3,1},{5,7},{10,8},{12,14},{11,9},{13,15},{18,16},{20,... | collective-permute-start | bytes 1572872 | tf_op jit(solution)/shard_map/ppermute | solution.py:431
  40.1 5.2 %collective-permute-start.5 = (bf16[128,2,256]{2,1,0:T(2,128)(2,1)S(1)}, bf16[128,2,256]{2,1,0:T(2,128)(2,1)S(1)}, u32[]{:S(2)}, u32[]{:S(2)}) collective-permute-start(bf16[128,2,256]{2,1,0:T(2,128)(2,1)S(1)} %slice.17), channel_id=1, source_target_pairs={{2,6},{3,7},{10,14},{11,15},{18,22},{19,23},{26,30},{27,31}} | collective-permute-start | bytes 393224 | tf_op jit(solution)/shard_map/ppermute | solution.py:425
  40.8 22.2 %collective-permute-start.3 = (bf16[512,256]{1,0:T(8,128)(2,1)S(1)}, bf16[512,256]{1,0:T(8,128)(2,1)S(1)}, u32[]{:S(2)}, u32[]{:S(2)}) collective-permute-start(bf16[512,256]{1,0:T(8,128)(2,1)S(1)} %pad_maximum_fusion), channel_id=1, source_target_pairs={{2,4},{4,2},{3,5},{5,3},{10,12},{12,10},{11,13},{13,11},{18,20},{2... | collective-permute-start | bytes 786440 | tf_op jit(solution)/shard_map/ppermute | solution.py:434
  49.4 19.0 %collective-permute-start.9 = (bf16[512,256]{1,0:T(8,128)(2,1)S(1)}, bf16[512,256]{1,0:T(8,128)(2,1)S(1)}, u32[]{:S(2)}, u32[]{:S(2)}) collective-permute-start(bf16[512,256]{1,0:T(8,128)(2,1)S(1)} %collective-permute-done.8.refs_0_), channel_id=1, source_target_pairs={{2,0},{4,6},{3,1},{5,7},{10,8},{12,14},{11,9},{13,15},{18,16},{20,... | collective-permute-start | bytes 786440 | tf_op jit(solution)/shard_map/ppermute | solution.py:447
  63.0 8.4 %collective-permute-start.6 = (bf16[512,256]{1,0:T(8,128)(2,1)S(1)}, bf16[512,256]{1,0:T(8,128)(2,1)S(1)}, u32[]{:S(2)}, u32[]{:S(2)}) collective-permute-start(bf16[512,256]{1,0:T(8,128)(2,1)S(1)} %collective-permute-done.3.refs_0_), channel_id=1, source_target_pairs={{2,0},{4,6},{3,1},{5,7},{10,8},{12,14},{11,9},{13,15},{18,16},{20,... | collective-permute-start | bytes 786440 | tf_op jit(solution)/shard_map/ppermute | solution.py:447

commit v4 on v2

--- a/solution.py
+++ b/solution.py
@@ -195,14 +195,17 @@
 
 
 def cross_kernel(
-    lengths_ref, images_ref, place_ref, q_ref, *refs, kv_heads, group, sources, samples, begin, end
+    lengths_ref, images_ref, place_ref, q_ref, *refs, kv_heads, group, sources, samples, begin, end, heads
 ):
     refs = list(refs)
     take = lambda n: [refs.pop(0) for _ in range(n)]
     pieces = [take(len(source)) for source in sources]
     stat_in, mixed_in = (None, None) if begin else take(2)
+    if end and heads[0] > 0:
+        take(1)
     out_ref = take(1)[0] if end else None
     stat_ref, mixed_ref, keys_ref, flipped_ref = take(4)
+    rows_ref, copied = take(2) if end else (None, None)
     rows_here = q_ref.shape[0]
     tiles = rows_here // TILE
     height = group * TILE
@@ -211,22 +214,19 @@
     image_count = keys_ref.shape[0]
 
     def fill(ref, at, row, parts, each):
-        for part in range(parts):
+        held = ref.shape[1] // HD // 2
+        for n, g in enumerate(heads):
+            k_at = (g if held == kv_heads else n) * HD
+            v_at = k_at + held * HD
             for image in range(image_count):
-                rows = slice(row + (part * image_count + image) * each, None)
-                rows = slice(rows.start, rows.start + each)
-                here = slice(at + part * each, at + (part + 1) * each)
-                for g in range(kv_heads):
-                    keys_ref[image, g, here] = ref[rows, g * HD : (g + 1) * HD]
-        for image in range(image_count):
-            for g in range(kv_heads):
-                column = (kv_heads + g) * HD
-                values = [
-                    ref[pl.ds(row + (part * image_count + image) * each, each), column : column + HD]
-                    for part in range(parts)
-                ]
+                values = []
+                for part in range(parts):
+                    first = row + (part * image_count + image) * each
+                    here = slice(at + part * each, at + (part + 1) * each)
+                    keys_ref[image, n, here] = ref[first : first + each, k_at : k_at + HD]
+                    values.append(ref[first : first + each, v_at : v_at + HD])
                 whole = jnp.concatenate(values, axis=0)
-                flipped_ref[image, g, :, at : at + parts * each] = whole.T
+                flipped_ref[image, n, :, at : at + parts * each] = whole.T
 
     at = 0
     for source, given in zip(sources, pieces):
@@ -259,19 +259,22 @@
         return [jnp.where(mine, n, o) for n, o in zip(new, old)]
 
     marks = [images_of(tile) for tile in range(tiles)]
-
-    def scores(tile, g):
-        return scores_of(keys_ref[marks[tile][1], g], stacked_queries(q_ref, tile, g, group))
-
-    def finish(tile, g, s):
+    order = range(len(heads))
+
+    def scores(tile, n):
+        return scores_of(
+            keys_ref[marks[tile][1], n], stacked_queries(q_ref, tile, heads[n], group)
+        )
+
+    def finish(tile, n, s):
         row_image, leading = marks[tile]
-        old = None
+        old, g = None, heads[n]
         if not begin:
             old = stat_in[tile, g, 0:1, :], stat_in[tile, g, 1:2, :], mixed_in[tile, g]
-        new = absorb(old, s, flipped_ref[leading, g])
-        keep(tile, g, chosen(row_image == leading, new, old))
-
-    staggered([(tile, g) for tile in range(tiles) for g in range(kv_heads)], scores, finish)
+        new = absorb(old, s, flipped_ref[leading, n])
+        keep(tile, n, chosen(row_image == leading, new, old))
+
+    staggered([(tile, n) for tile in range(tiles) for n in order], scores, finish)
 
     @pl.loop(0, tiles)
     def _(tile):
@@ -289,21 +292,36 @@
             def _(image=image):
                 row_image, _ = images_of(tile)
                 olds = [
-                    (stat_ref[tile, g, 0:1, :], stat_ref[tile, g, 1:2, :], mixed_ref[tile, g])
-                    for g in range(kv_heads)
+                    (stat_ref[tile, n, 0:1, :], stat_ref[tile, n, 1:2, :], mixed_ref[tile, n])
+                    for n in order
                 ]
                 ss = [
-                    scores_of(keys_ref[image, g], stacked_queries(q_ref, tile, g, group))
-                    for g in range(kv_heads)
+                    scores_of(keys_ref[image, n], stacked_queries(q_ref, tile, heads[n], group))
+                    for n in order
                 ]
-                for g in range(kv_heads):
-                    new = absorb(olds[g], ss[g], flipped_ref[image, g])
-                    keep(tile, g, chosen(row_image == image, new, olds[g]))
-
-    if end:
-        for tile in range(tiles):
-            for g in range(kv_heads):
-                write_heads(out_ref, mixed_ref[tile, g], stat_ref[tile, g, 1:2, :], tile, g, group)
+                for n in order:
+                    new = absorb(olds[n], ss[n], flipped_ref[image, n])
+                    keep(tile, n, chosen(row_image == image, new, olds[n]))
+
+    if not end:
+        return
+    share = len(heads) * group * HD
+    pace = 2
+    copies = []
+    for tile in range(tiles):
+        for n in order:
+            write_heads(rows_ref, mixed_ref[tile, n], stat_ref[tile, n, 1:2, :], tile, n, group)
+        if (tile + 1) % pace == 0 or tile + 1 == tiles:
+            done = slice(len(copies) * pace * TILE, (tile + 1) * TILE)
+            copy = pltpu.make_async_copy(
+                rows_ref.at[done],
+                out_ref.at[done, heads[0] * group * HD : heads[0] * group * HD + share],
+                copied.at[len(copies)],
+            )
+            copy.start()
+            copies.append(copy)
+    for copy in copies:
+        copy.wait()
 
 
 def smem():
@@ -321,12 +339,35 @@
     )
 
 
+def join_kernel(passed_ref, rows_ref, out_ref):
+    half = passed_ref.shape[0] // 2
+    count = rows_ref.shape[0]
+    out_ref[:half] = passed_ref[half:]
+    out_ref[half : half + count] = rows_ref[...]
+    out_ref[half + count :] = passed_ref[:half]
+
+
+def joined(passed, own_rows):
+    total, width = passed.shape[0] + own_rows.shape[0], passed.shape[1]
+    return pl.pallas_call(
+        join_kernel,
+        out_shape=jax.ShapeDtypeStruct((total, width), passed.dtype),
+        in_specs=[vmem(), vmem()],
+        out_specs=vmem(),
+        cost_estimate=pl.CostEstimate(
+            flops=0, bytes_accessed=4 * total * width, transcendentals=0
+        ),
+    )(passed, own_rows)
+
+
 def state_shapes(rows, kv_heads, group):
     tiles, height = rows // TILE, group * TILE
     return (tiles, kv_heads, 8, height), (tiles, kv_heads, HD, height)
 
 
-def state_call(kernel, operands, rows, width, keys, shapes, scratch, end, dtype):
+def state_call(
+    kernel, operands, rows, width, keys, shapes, scratch, end, dtype, placed=False, rest=None
+):
     scalars = sum(x.dtype == jnp.int32 for x in operands)
     state_scratch = []
     if end:
@@ -334,12 +375,19 @@
         state_scratch = [pltpu.VMEM(s, jnp.float32) for s in shapes]
     else:
         out_shape = [jax.ShapeDtypeStruct(s, jnp.float32) for s in shapes]
+    anywhere = pl.BlockSpec(memory_space=pl.ANY)
+    in_specs = [smem()] * scalars + [vmem()] * (len(operands) - scalars)
+    aliases = {}
+    if rest is not None:
+        aliases = {len(operands): 0}
+        operands, in_specs = (*operands, rest), in_specs + [anywhere]
     return pl.pallas_call(
         kernel,
         out_shape=out_shape,
-        in_specs=[smem()] * scalars + [vmem()] * (len(operands) - scalars),
-        out_specs=vmem() if end else [vmem(), vmem()],
+        in_specs=in_specs,
+        out_specs=(anywhere if placed else vmem()) if end else [vmem(), vmem()],
         scratch_shapes=state_scratch + scratch,
+        input_output_aliases=aliases,
         compiler_params=pltpu.CompilerParams(vmem_limit_bytes=28 << 20),
         cost_estimate=cost(rows, width, keys),
     )(*operands)
@@ -361,62 +409,34 @@
     return state_call(kernel, operands, rows, width, keys, shapes, scratch, end, q.dtype)
 
 
-def cross_attention(lengths, images, place, q, sources, state, end, kv_heads, group, image_count):
+def cross_attention(
+    lengths, images, place, q, sources, state, end, kv_heads, group, image_count,
+    heads=None, rest=None,
+):
+    heads = tuple(range(kv_heads)) if heads is None else heads
     rows, width = q.shape
     begin = state is None
     kernel = functools.partial(
-        cross_kernel, kv_heads=kv_heads, group=group,
+        cross_kernel, kv_heads=kv_heads, group=group, heads=heads,
         sources=tuple(tuple(piece[1:] for piece in source) for source in sources),
         samples=lengths.shape[1], begin=begin, end=end,
     )
     pieces = [piece[0] for source in sources for piece in source]
     keys = sum(source[0][2] * source[0][3] for source in sources)
     scratch = [
-        pltpu.VMEM((image_count, kv_heads, keys, HD), q.dtype),
-        pltpu.VMEM((image_count, kv_heads, HD, keys), q.dtype),
+        pltpu.VMEM((image_count, len(heads), keys, HD), q.dtype),
+        pltpu.VMEM((image_count, len(heads), HD, keys), q.dtype),
     ]
+    if end:
+        scratch += [
+            pltpu.VMEM((rows, len(heads) * group * HD), q.dtype),
+            pltpu.SemaphoreType.DMA((rows // TILE,)),
+        ]
     operands = (lengths, images, place, q, *pieces, *(() if begin else state))
-    shapes = state_shapes(rows, kv_heads, group)
-    return state_call(kernel, operands, rows, width, keys, shapes, scratch, end, q.dtype)
-
-
-def cross_ending(lengths, images, place, q, sources, state, rest, head, kv_heads, group, image_count):
-    rows, width = q.shape
-    share = width // kv_heads
-    keys = sources[0][2] * sources[0][3]
-    kernel = functools.partial(
-        cross_kernel, kv_heads=1, group=group,
-        sources=(tuple(piece[1:] for piece in sources),),
-        samples=lengths.shape[1], begin=False, end=True,
-    )
-    pieces = [piece[0] for piece in sources]
-    shapes = state_shapes(rows, 1, group)
-    first = lambda shape: pl.BlockSpec(shape, lambda i: (0, head) + (0,) * (len(shape) - 2))
-    body = lambda *refs: kernel(*refs)
-    operands = [lengths, images, place, q, *pieces, *state]
-    in_specs = [smem()] * 3 + [first((rows, share))] + [vmem()] * len(pieces)
-    in_specs += [first(shape) for shape in shapes]
-    aliases = {}
-    if rest is not None:
-        body = lambda *refs: kernel(*refs[: len(operands) - 1], *refs[len(operands) :])
-        aliases = {len(operands): 0}
-        operands.append(rest)
-        in_specs.append(pl.BlockSpec(memory_space=pl.ANY))
-    return pl.pallas_call(
-        body,
-        out_shape=jax.ShapeDtypeStruct((rows, width), q.dtype),
-        grid=(1,),
-        in_specs=in_specs,
-        out_specs=first((rows, share)),
-        scratch_shapes=[pltpu.VMEM(s, jnp.float32) for s in shapes]
-        + [
-            pltpu.VMEM((image_count, 1, keys, HD), q.dtype),
-            pltpu.VMEM((image_count, 1, HD, keys), q.dtype),
-        ],
-        input_output_aliases=aliases,
-        compiler_params=pltpu.CompilerParams(vmem_limit_bytes=28 << 20),
-        cost_estimate=cost(rows, share, keys),
-    )(*operands)
+    shapes = state_shapes(rows, len(heads), group)
+    return state_call(
+        kernel, operands, rows, width, keys, shapes, scratch, end, q.dtype, True, rest
+    )
 
 
 def per_device(q_self, kv_self, q_cross, kv_cross, sample_lengths, sample_image, *, n_pipe, n_ctx):
@@ -449,7 +469,7 @@
     )
     if n_ctx == 4:
         half = rows // 2
-        block = jnp.concatenate([passed[half:], own_rows, passed[:half]], axis=0)
+        block = joined(passed, own_rows)
         at = lambda array, row: (array, row, n_pipe, each)
         near = lax.ppermute(block, "ctx", [(1, 2), (2, 1)])
         pair = lax.ppermute(block, "ctx", [(0, 1), (1, 0), (2, 3), (3, 2)])
@@ -457,7 +477,8 @@
         parts = ((0, 0, 0, 0, rows, None), (1, 1, 0, 0, rows, None))
         state = attend_cross([[at(own_rows, 0)]], None, False)
         self_state = attend_self([own, passed], early, parts, None, False)
-        near, pair, state, self_state = lax.optimization_barrier((near, pair, state, self_state))
+        near, state = lax.optimization_barrier((near, state))
+        pair, self_state = lax.optimization_barrier((pair, self_state))
         columns = lambda j: pair[half : half + cross_rows, j * HD : (j + 1) * HD]
         far = [
             lax.ppermute(
@@ -484,10 +505,8 @@
         self_out = attend_self([near_on], ((3, half),), parts, self_state, True)
         cross_out = None
         for g in range(kv_heads):
-            cross_out = cross_ending(
-                sample_lengths, sample_image, place, q_cross[0],
-                [at(far[g], 0), at(far_on[g], 0)], state, cross_out, g,
-                kv_heads, group, image_count,
+            cross_out = attend_cross(
+                [[at(far[g], 0), at(far_on[g], 0)]], state, True, heads=(g,), rest=cross_out
             )
     else:
         pieces, spans, left, step = [own, passed], [(0, rows), (1, rows)], longest - 1 - rows, 1

time: 75.6 us -> 74.8 us (0.989)
  starting transfers between devices: 17 us -> 20.1 us
  waiting for transfers between devices: 21.7 us -> 19.6 us
  local copies, waits for them, and re-layouts: 3.63 us -> 1.81 us
    ppermute x1, starting transfers between devices: 2.38 us -> 5.21 us  [per_device(): pair = lax.ppermute(block, 'ctx', [(0, 1), (1, 0), (2, 3), (3, 2)])]
    ppermute x1, waiting for transfers between devices: 9.45 us -> 6.88 us  [per_device(): near_on = lax.ppermute(near[:half + cross_rows], 'ctx', [(1, 0), (2, 3)])]
    unnamed x15 -> x17, local copies, waits for them, and re-layouts: 2.65 us -> 1.67 us
    pallas_call x8 -> x9, Pallas kernels: 33.3 us -> 33.1 us  [the longest x8 31 us: state_call(): pl.pallas_call(kernel, out_shape=out_shape, in_specs=in_specs, out_specs=...]
  transfers between devices with their start and end apart: 9 -> 9, of which waited for: 3 -> 3; matrix products, arithmetic and copies ran while one was open for 2% -> 0% of each run, Pallas kernels for 37% -> 35%
where the time goes in v4:
time: 74.8 us; the launch traced here: 75.8 us
  Pallas kernels  33.1 us (44%)
  starting transfers between devices  20.1 us (27%)
  waiting for transfers between devices  19.6 us (26%)
  local copies, waits for them, and re-layouts  1.81 us (2%)
  between operations  1.01 us (1%)
    pallas_call x8, Pallas kernels, state_call(): pl.pallas_call(kernel, out_shape=out_shape, in_specs=in_specs, out_specs=...  31 us
    ppermute x1, waiting for transfers between devices, per_device(): pair = lax.ppermute(block, 'ctx', [(0, 1), (1, 0), (2, 3), (3, 2)])  7.1 us
    ppermute x1, waiting for transfers between devices, per_device(): near_on = lax.ppermute(near[:half + cross_rows], 'ctx', [(1, 0), (2, 3)])  6.88 us
    ppermute x1, waiting for transfers between devices, per_device(): lax.ppermute(piece, 'ctx', [(c, c + 1) for c in range(step - 1, n_ctx - 1)])  5.63 us
    all_to_all x1, starting transfers between devices, per_device(): lax.all_to_all(kv_cross, 'pipe', split_axis=0, concat_axis=0, tiled=True)  5.31 us
    ppermute x1, starting transfers between devices, per_device(): pair = lax.ppermute(block, 'ctx', [(0, 1), (1, 0), (2, 3), (3, 2)])  5.21 us
    ppermute x1, starting transfers between devices, per_device(): lax.ppermute(piece, 'ctx', [(c, c + 1) for c in range(step - 1, n_ctx - 1)])  3.63 us
    ppermute x2, starting transfers between devices, per_device(): far_on = [lax.ppermute(part, 'ctx', [(1, 0), (2, 3)]) for part in far]  2.58 us
  transfers between devices with their start and end apart: 9, of which 3 were waited for; matrix products, arithmetic and copies ran while one was open for 0% of the time, Pallas kernels for 35%

profile of v4, /device:TPU:0, one launch (start us, length us, event | category | flops | bytes accessed | tf_op | source)
XLA Modules:
  0.0 75.8 jit_solution(13206805836958175561)
XLA Ops:
  0.6 0.0 copy-start.6
  0.6 5.3 %all-to-all-start = ((bf16[4,2,64,2,256]{4,3,2,1,0:T(2,128)(2,1)}), bf16[4,2,64,2,256]{4,3,2,1,0:T(2,128)(2,1)S(1)}, u32[]{:S(2)}, u32[]{:S(2)}) async-start(bf16[4,2,64,2,256]{4,3,2,1,0:T(2,128)(2,1)} %param.9), calls=%async_computation | async-start | bytes 1048576 | tf_op jit(solution)/shard_map/all_to_all | solution.py:455
  5.9 0.0 copy-start
  5.9 0.0 copy-start.4
  6.0 0.0 copy-start.5
  6.0 3.6 %collective-permute-start = (bf16[256,2,256]{2,1,0:T(2,128)(2,1)}, bf16[256,2,256]{2,1,0:T(2,128)(2,1)S(1)}, u32[]{:S(2)}, u32[]{:S(2)}) collective-permute-start(bf16[256,2,256]{2,1,0:T(2,128)(2,1)} %bitcast.31), channel_id=1, source_target_pairs={{0,2},{2,4},{4,6},{1,3},{3,5},{5,7},{8,10},{10,12},{12,14},{9,11},... | collective-permute-start | bytes 786440 | tf_op jit(solution)/shard_map/ppermute | solution.py:451
  9.6 5.6 %collective-permute-done = bf16[256,2,256]{2,1,0:T(2,128)(2,1)S(1)} collective-permute-done((bf16[256,2,256]{2,1,0:T(2,128)(2,1)}, bf16[256,2,256]{2,1,0:T(2,128)(2,1)S(1)}, u32[]{:S(2)}, u32[]{:S(2)}) %collective-permute-start) | collective-permute-done | bytes 262176 | tf_op jit(solution)/shard_map/ppermute | solution.py:451
  15.2 0.0 all-to-all-done
  15.2 0.7 copy.9
  16.0 0.9 %copy.10 = bf16[64,8,2,256]{3,1,2,0:T(8,128)(2,1)} copy(bf16[64,8,2,256]{3,2,1,0:T(2,128)(2,1)S(1)} %bitcast.29) | data formatting | bytes 1048576
  16.8 0.0 copy-start.2
  16.8 2.1 %shard_map.77 = bf16[768,512]{1,0:T(8,128)(2,1)} custom-call(bf16[256,512]{1,0:T(8,128)(2,1)} %bitcast.25, bf16[512,512]{1,0:T(8,128)(2,1)} %bitcast.23), custom_call_target="tpu_custom_call" | custom-call | bytes 1572864 | tf_op jit(solution)/shard_map/pallas_call | solution.py:352
  19.0 0.7 collective-permute-start.1
  19.7 5.2 %collective-permute-start.3 = (bf16[768,512]{1,0:T(8,128)(2,1)}, bf16[768,512]{1,0:T(8,128)(2,1)S(1)}, u32[]{:S(2)}, u32[]{:S(2)}) collective-permute-start(bf16[768,512]{1,0:T(8,128)(2,1)} %shard_map.77), channel_id=1, source_target_pairs={{0,2},{2,0},{4,6},{6,4},{1,3},{3,1},{5,7},{7,5},{8,10},{10,8},{12,... | collective-permute-start | bytes 2359304 | tf_op jit(solution)/shard_map/ppermute | solution.py:475
  24.9 0.0 copy-done.6
  24.9 0.0 copy-start.1
  24.9 0.0 copy-start.3
  24.9 0.1 pad_add_fusion.place_ref
  25.0 0.0 copy-done
  25.0 0.0 copy-done.4
  25.0 0.0 copy-done.5
  25.0 0.0 copy-done.2
  25.0 5.2 %shard_map.78 = (f32[8,2,8,256]{3,2,1,0:T(8,128)S(1)}, f32[8,2,128,256]{3,2,1,0:T(8,128)S(1)}) custom-call(s32[1,8]{1,0:T(1,128)S(1)} %copy-done.4, s32[1,8]{1,0:T(1,128)S(1)} %copy-done.5, s32[2]{0:T(128)S(1)} %pad_add_fusion.place_ref, bf16[256,2048]{1,0:T(8,128)(2,1)S(1)} %bitcast.15, bf16[512,512]{1,0:T(8,128)(2,1)S(1)} %bitcast.24), custom_call_target="tpu_custom_call" | custom-call | flops 1073741824 | bytes 2097152 | tf_op jit(solution)/shard_map/pallas_call | solution.py:384
  30.2 0.0 copy-done.1
  30.2 0.0 copy-done.3
  30.2 2.5 %shard_map.79 = (f32[8,2,8,256]{3,2,1,0:T(8,128)S(1)}, f32[8,2,128,256]{3,2,1,0:T(8,128)S(1)}) custom-call(s32[1,8]{1,0:T(1,128)S(1)} %copy-done.4, s32[2]{0:T(128)S(1)} %pad_add_fusion.place_ref, bf16[256,2048]{1,0:T(8,128)(2,1)S(1)} %bitcast.20, bf16[256,512]{1,0:T(8,128)(2,1)S(1)} %bitcast.27, bf16[256,512]{1,0:T(8,128)(2,1)S(1)} %bitcast.26), custom_call_target="tpu_custom_call" | custom-call | flops 2147483648 | bytes 2097152 | tf_op jit(solution)/shard_map/pallas_call | solution.py:384
  32.8 0.0 collective-permute-done.1.refs_0_
  32.8 1.3 %collective-permute-start.2 = (bf16[640,512]{1,0:T(8,128)(2,1)S(1)}, bf16[640,512]{1,0:T(8,128)(2,1)S(1)}, u32[]{:S(2)}, u32[]{:S(2)}) collective-permute-start(bf16[640,512]{1,0:T(8,128)(2,1)S(1)} %slice.15), channel_id=1, source_target_pairs={{2,0},{4,6},{3,1},{5,7},{10,8},{12,14},{11,9},{13,15},{18,16},{20,... | collective-permute-start | bytes 1966088 | tf_op jit(solution)/shard_map/ppermute | solution.py:490
  34.1 7.1 %collective-permute-done.3.refs_1_.refs_0_ = bf16[768,512]{1,0:T(8,128)(2,1)S(1)} collective-permute-done((bf16[768,512]{1,0:T(8,128)(2,1)}, bf16[768,512]{1,0:T(8,128)(2,1)S(1)}, u32[]{:S(2)}, u32[]{:S(2)}) %collective-permute-start.3) | collective-permute-done | bytes 786464 | tf_op jit(solution)/shard_map/ppermute | solution.py:475
  41.2 0.1 fusion
  41.4 0.7 collective-permute-start.6
  42.1 0.7 collective-permute-start.4
  42.8 5.3 %shard_map.82 = (f32[8,2,8,256]{3,2,1,0:T(8,128)S(1)}, f32[8,2,128,256]{3,2,1,0:T(8,128)S(1)}) custom-call(s32[1,8]{1,0:T(1,128)S(1)} %copy-done.4, s32[1,8]{1,0:T(1,128)S(1)} %copy-done.5, s32[2]{0:T(128)S(1)} %pad_add_fusion.place_ref, bf16[256,2048]{1,0:T(8,128)(2,1)S(1)} %bitcast.16, bf16[768,512]{1,0:T(8,128)(2,1)S(1)} %collective-permute-done.3.refs_1_.refs_0_, ...), custom_call_target="tpu_custom_call" | custom-call | flops 1073741824 | bytes 2097152 | tf_op jit(solution)/shard_map/pallas_call | solution.py:384
  48.1 0.0 collective-permute-done.6.refs_0_
  48.1 1.3 %collective-permute-start.7 = (bf16[512,256]{1,0:T(8,128)(2,1)S(1)}, bf16[512,256]{1,0:T(8,128)(2,1)S(1)}, u32[]{:S(2)}, u32[]{:S(2)}) collective-permute-start(bf16[512,256]{1,0:T(8,128)(2,1)S(1)} %collective-permute-done.6.refs_0_), channel_id=1, source_target_pairs={{2,0},{4,6},{3,1},{5,7},{10,8},{12,14},{11,9},{13,15},{18,16},{20,... | collective-permute-start | bytes 786440 | tf_op jit(solution)/shard_map/ppermute | solution.py:502
  49.4 1.0 %shard_map.80 = (f32[8,2,8,256]{3,2,1,0:T(8,128)S(1)}, f32[8,2,128,256]{3,2,1,0:T(8,128)S(1)}) custom-call(s32[1,8]{1,0:T(1,128)S(1)} %copy-done.4, s32[2]{0:T(128)S(1)} %pad_add_fusion.place_ref, bf16[256,2048]{1,0:T(8,128)(2,1)S(1)} %bitcast.21, bf16[768,512]{1,0:T(8,128)(2,1)S(1)} %collective-permute-done.1.refs_0_, ...), custom_call_target="tpu_custom_call" | custom-call | flops 1073741824 | bytes 2097152 | tf_op jit(solution)/shard_map/pallas_call | solution.py:384
  50.4 0.0 collective-permute-done.4.refs_0_
  50.4 1.3 %collective-permute-start.5 = (bf16[512,256]{1,0:T(8,128)(2,1)S(1)}, bf16[512,256]{1,0:T(8,128)(2,1)S(1)}, u32[]{:S(2)}, u32[]{:S(2)}) collective-permute-start(bf16[512,256]{1,0:T(8,128)(2,1)S(1)} %collective-permute-done.4.refs_0_), channel_id=1, source_target_pairs={{2,0},{4,6},{3,1},{5,7},{10,8},{12,14},{11,9},{13,15},{18,16},{20,... | collective-permute-start | bytes 786440 | tf_op jit(solution)/shard_map/ppermute | solution.py:502
  51.7 6.9 %collective-permute-done.2.refs_0_.refs_1_ = bf16[640,512]{1,0:T(8,128)(2,1)S(1)} collective-permute-done((bf16[640,512]{1,0:T(8,128)(2,1)S(1)}, bf16[640,512]{1,0:T(8,128)(2,1)S(1)}, u32[]{:S(2)}, u32[]{:S(2)}) %collective-permute-start.2) | collective-permute-done | bytes 655392 | tf_op jit(solution)/shard_map/ppermute | solution.py:490
  58.6 2.1 %shard_map.81 = bf16[256,2048]{1,0:T(8,128)(2,1)} custom-call(s32[1,8]{1,0:T(1,128)S(1)} %copy-done.4, s32[2]{0:T(128)S(1)} %pad_add_fusion.place_ref, bf16[256,2048]{1,0:T(8,128)(2,1)S(1)} %bitcast.22, bf16[640,512]{1,0:T(8,128)(2,1)S(1)} %collective-permute-done.2.refs_0_.refs_1_, f32[8,2,8,256]{3,2,1,0:T(8,128)S(1)} %get-tuple-element.38.refs_1_, ...), custom_call_target="tpu_custom_call" | custom-call | flops 536870912 | bytes 2097152 | tf_op jit(solution)/shard_map/pallas_call | solution.py:384
  60.6 5.4 %shard_map.83 = (f32[8,2,8,256]{3,2,1,0:T(8,128)S(1)}, f32[8,2,128,256]{3,2,1,0:T(8,128)S(1)}) custom-call(s32[1,8]{1,0:T(1,128)S(1)} %copy-done.4, s32[1,8]{1,0:T(1,128)S(1)} %copy-done.5, s32[2]{0:T(128)S(1)} %pad_add_fusion.place_ref, bf16[256,2048]{1,0:T(8,128)(2,1)S(1)} %bitcast.17, bf16[768,512]{1,0:T(8,128)(2,1)S(1)} %collective-permute-done.1.refs_0_, ...), custom_call_target="tpu_custom_call" | custom-call | flops 1073741824 | bytes 2097152 | tf_op jit(solution)/shard_map/pallas_call | solution.py:384
  66.0 0.0 collective-permute-done.7.refs_1_
  66.0 4.8 %shard_map.84.refs_4_ = bf16[256,2048]{1,0:T(8,128)(2,1)} custom-call(s32[1,8]{1,0:T(1,128)S(1)} %copy-done.4, s32[1,8]{1,0:T(1,128)S(1)} %copy-done.5, s32[2]{0:T(128)S(1)} %pad_add_fusion.place_ref, bf16[256,2048]{1,0:T(8,128)(2,1)S(1)} %bitcast.18, bf16[512,256]{1,0:T(8,128)(2,1)S(1)} %collective-permute-done.6.refs_0_, ...), custom_call_target="tpu_custom_call" | custom-call | flops 1073741824 | bytes 2097152 | tf_op jit(solution)/shard_map/pallas_call | solution.py:384
  70.8 0.0 collective-permute-done.5.refs_1_
  70.8 4.8 %shard_map.85 = bf16[256,2048]{1,0:T(8,128)(2,1)} custom-call(s32[1,8]{1,0:T(1,128)S(1)} %copy-done.4, s32[1,8]{1,0:T(1,128)S(1)} %copy-done.5, s32[2]{0:T(128)S(1)} %pad_add_fusion.place_ref, bf16[256,2048]{1,0:T(8,128)(2,1)S(1)} %bitcast.19, bf16[512,256]{1,0:T(8,128)(2,1)S(1)} %collective-permute-done.4.refs_0_, ...), custom_call_target="tpu_custom_call", output_to_operand_aliasing={{}: (8, {})} | custom-call | flops 1073741824 | bytes 2097152 | tf_op jit(solution)/shard_map/pallas_call | solution.py:384
  (4 shorter events, 0.1 us)
Async XLA Ops:
  0.6 24.2 %copy-start.6 = (bf16[1,256,2,256]{3,2,1,0:T(2,128)(2,1)S(1)}, bf16[1,256,2,256]{3,2,1,0:T(2,128)(2,1)}, u32[]{:S(2)}) copy-start(bf16[1,256,2,256]{3,2,1,0:T(2,128)(2,1)} %param.7) | copy-start | bytes 786436
  0.6 14.6 %all-to-all-start = ((bf16[4,2,64,2,256]{4,3,2,1,0:T(2,128)(2,1)}), bf16[4,2,64,2,256]{4,3,2,1,0:T(2,128)(2,1)S(1)}, u32[]{:S(2)}, u32[]{:S(2)}) async-start(bf16[4,2,64,2,256]{4,3,2,1,0:T(2,128)(2,1)} %param.9), calls=%async_computation | async-start | bytes 1048576 | tf_op jit(solution)/shard_map/all_to_all | solution.py:455
  5.9 19.1 %copy-start = (bf16[1,256,2048]{2,1,0:T(8,128)(2,1)S(1)}, bf16[1,256,2048]{2,1,0:T(8,128)(2,1)}, u32[]{:S(2)}) copy-start(bf16[1,256,2048]{2,1,0:T(8,128)(2,1)} %param.8) | copy-start | bytes 3145732
  5.9 19.1 %copy-start.4 = (s32[1,8]{1,0:T(1,128)S(1)}, s32[1,8]{1,0:T(1,128)}, u32[]{:S(2)}) copy-start(s32[1,8]{1,0:T(1,128)} %lengths_ref.15) | copy-start | bytes 100
  6.0 19.1 %copy-start.5 = (s32[1,8]{1,0:T(1,128)S(1)}, s32[1,8]{1,0:T(1,128)}, u32[]{:S(2)}) copy-start(s32[1,8]{1,0:T(1,128)} %images_ref.9) | copy-start | bytes 100
  6.0 9.3 %collective-permute-start = (bf16[256,2,256]{2,1,0:T(2,128)(2,1)}, bf16[256,2,256]{2,1,0:T(2,128)(2,1)S(1)}, u32[]{:S(2)}, u32[]{:S(2)}) collective-permute-start(bf16[256,2,256]{2,1,0:T(2,128)(2,1)} %bitcast.31), channel_id=1, source_target_pairs={{0,2},{2,4},{4,6},{1,3},{3,5},{5,7},{8,10},{10,12},{12,14},{9,11},... | collective-permute-start | bytes 786440 | tf_op jit(solution)/shard_map/ppermute | solution.py:451
  16.8 8.2 %copy-start.2 = (bf16[64,8,2,256]{3,1,2,0:T(8,128)(2,1)S(1)}, bf16[64,8,2,256]{3,1,2,0:T(8,128)(2,1)}, u32[]{:S(2)}) copy-start(bf16[64,8,2,256]{3,1,2,0:T(8,128)(2,1)} %copy.10) | copy-start | bytes 1572868
  19.0 13.8 %collective-permute-start.1 = (bf16[768,512]{1,0:T(8,128)(2,1)}, bf16[768,512]{1,0:T(8,128)(2,1)S(1)}, u32[]{:S(2)}, u32[]{:S(2)}) collective-permute-start(bf16[768,512]{1,0:T(8,128)(2,1)} %shard_map.77), channel_id=1, source_target_pairs={{2,4},{4,2},{3,5},{5,3},{10,12},{12,10},{11,13},{13,11},{18,20},{2... | collective-permute-start | bytes 2359304 | tf_op jit(solution)/shard_map/ppermute | solution.py:474
  19.7 21.6 %collective-permute-start.3 = (bf16[768,512]{1,0:T(8,128)(2,1)}, bf16[768,512]{1,0:T(8,128)(2,1)S(1)}, u32[]{:S(2)}, u32[]{:S(2)}) collective-permute-start(bf16[768,512]{1,0:T(8,128)(2,1)} %shard_map.77), channel_id=1, source_target_pairs={{0,2},{2,0},{4,6},{6,4},{1,3},{3,1},{5,7},{7,5},{8,10},{10,8},{12,... | collective-permute-start | bytes 2359304 | tf_op jit(solution)/shard_map/ppermute | solution.py:475
  24.9 5.3 %copy-start.1 = (bf16[1,256,2048]{2,1,0:T(8,128)(2,1)S(1)}, bf16[1,256,2048]{2,1,0:T(8,128)(2,1)}, u32[]{:S(2)}) copy-start(bf16[1,256,2048]{2,1,0:T(8,128)(2,1)} %param.6) | copy-start | bytes 3145732
  24.9 5.3 %copy-start.3 = (bf16[32,8,2,256]{3,1,2,0:T(8,128)(2,1)S(1)}, bf16[32,8,2,256]{3,1,2,0:T(8,128)(2,1)}, u32[]{:S(2)}) copy-start(bf16[32,8,2,256]{3,1,2,0:T(8,128)(2,1)} %copy.9) | copy-start | bytes 786436
  32.8 25.7 %collective-permute-start.2 = (bf16[640,512]{1,0:T(8,128)(2,1)S(1)}, bf16[640,512]{1,0:T(8,128)(2,1)S(1)}, u32[]{:S(2)}, u32[]{:S(2)}) collective-permute-start(bf16[640,512]{1,0:T(8,128)(2,1)S(1)} %slice.15), channel_id=1, source_target_pairs={{2,0},{4,6},{3,1},{5,7},{10,8},{12,14},{11,9},{13,15},{18,16},{20,... | collective-permute-start | bytes 1966088 | tf_op jit(solution)/shard_map/ppermute | solution.py:490
  41.4 6.7 %collective-permute-start.6 = (bf16[512,256]{1,0:T(8,128)(2,1)S(1)}, bf16[512,256]{1,0:T(8,128)(2,1)S(1)}, u32[]{:S(2)}, u32[]{:S(2)}) collective-permute-start(bf16[512,256]{1,0:T(8,128)(2,1)S(1)} %pad_maximum_fusion.1), channel_id=1, source_target_pairs={{2,4},{4,2},{3,5},{5,3},{10,12},{12,10},{11,13},{13,11},{18,20},{2... | collective-permute-start | bytes 786440 | tf_op jit(solution)/shard_map/ppermute | solution.py:484
  42.1 8.3 %collective-permute-start.4 = (bf16[512,256]{1,0:T(8,128)(2,1)S(1)}, bf16[512,256]{1,0:T(8,128)(2,1)S(1)}, u32[]{:S(2)}, u32[]{:S(2)}) collective-permute-start(bf16[512,256]{1,0:T(8,128)(2,1)S(1)} %pad_maximum_fusion), channel_id=1, source_target_pairs={{2,4},{4,2},{3,5},{5,3},{10,12},{12,10},{11,13},{13,11},{18,20},{2... | collective-permute-start | bytes 786440 | tf_op jit(solution)/shard_map/ppermute | solution.py:484
  48.1 17.9 %collective-permute-start.7 = (bf16[512,256]{1,0:T(8,128)(2,1)S(1)}, bf16[512,256]{1,0:T(8,128)(2,1)S(1)}, u32[]{:S(2)}, u32[]{:S(2)}) collective-permute-start(bf16[512,256]{1,0:T(8,128)(2,1)S(1)} %collective-permute-done.6.refs_0_), channel_id=1, source_target_pairs={{2,0},{4,6},{3,1},{5,7},{10,8},{12,14},{11,9},{13,15},{18,16},{20,... | collective-permute-start | bytes 786440 | tf_op jit(solution)/shard_map/ppermute | solution.py:502
  50.4 20.5 %collective-permute-start.5 = (bf16[512,256]{1,0:T(8,128)(2,1)S(1)}, bf16[512,256]{1,0:T(8,128)(2,1)S(1)}, u32[]{:S(2)}, u32[]{:S(2)}) collective-permute-start(bf16[512,256]{1,0:T(8,128)(2,1)S(1)} %collective-permute-done.4.refs_0_), channel_id=1, source_target_pairs={{2,0},{4,6},{3,1},{5,7},{10,8},{12,14},{11,9},{13,15},{18,16},{20,... | collective-permute-start | bytes 786440 | tf_op jit(solution)/shard_map/ppermute | solution.py:502
